TPU v7x, 512 devices: a whole 4x8x8 slice. The times are simulated.
512 devices in a mesh: vis: 64 (over z, x, core), txt: 8 (over y).
Axes of the slice: x: 4, y: 8, z: 8, core: 2. Of those that a mesh axis runs over, the one named last changes fastest.
Arguments:
- queries: bfloat16 [65536, 4096], P(('txt', 'vis')), may hold values from -6 to 6
- out_grad: bfloat16 [65536, 4096], P(('txt', 'vis')), may hold values from -6 to 6
- vision: bfloat16 [8, 384, 8192], P('txt', None, 'vis'), may hold values from -6 to 6
- w_kv: bfloat16 [8192, 1024], P('vis', 'txt'), may hold values from -1 to 1
- links: int32 [8, 64, 16], P('txt'), may hold values from 0 to 1, as said below
- img_count: int32 [8], P('txt'), may hold values from 1 to 16, as said below
Outputs:
- query_grad: bfloat16 [65536, 4096], P(('txt', 'vis'))
- vision_grad: bfloat16 [8, 384, 8192], P('txt', None, 'vis')
- w_kv_grad: float32 [8192, 1024], P('vis', 'txt')
Inputs may be any that keep to these rules, and one draw needn't show every extreme that they name: `links`: entries are 0 or 1; every block is linked to slot 0. `img_count`: slots at or past a document's count are not seen, whatever links says.
All inputs are finite; a program needn't handle non-finite values.
Results may differ from a plain program's by a relative error of at most 0.025.
Values may be sent and summed in bfloat16 or wider, within the bound.
A program may use at most 64 MiB of HBM per device.

v0:
```python
import jax
import jax.numpy as jnp
from jax import lax
from jax.sharding import PartitionSpec as P

HD = 128
QH = 32
KVH = 4
IMG_DOC = 16
IMG_LEN = 24
BLOCK = 128


def local(queries, out_grad, vision, w_kv, links, img_count):
    row_count = queries.shape[0]
    group_size = QH // KVH
    scaling = HD ** (-0.5)
    weight_full = lax.all_gather(w_kv, "txt", axis=1, tiled=True)
    images = vision[0]
    kv_width = weight_full.shape[1] // 2
    partial_value = jnp.dot(images, weight_full, preferred_element_type=jnp.float32)
    kv_pair = lax.psum(partial_value, "vis").astype(jnp.bfloat16)
    first_text = lax.axis_index("vis") * row_count
    block_ids = (first_text + jnp.arange(row_count, dtype=jnp.int32)) // BLOCK
    link_rows = jnp.take(links[0], block_ids, axis=0)
    image_ids = jnp.arange(IMG_DOC, dtype=jnp.int32)
    live_links = (link_rows == 1) & (image_ids[None, :] < img_count[0])
    allowed = jnp.repeat(live_links, IMG_LEN, axis=1)
    dq_parts = []
    key_parts = []
    value_parts = []
    for head_index in range(KVH):
        low = head_index * group_size * HD
        high = (head_index + 1) * group_size * HD
        query_head = queries[:, low:high].reshape(row_count, group_size, HD)
        grad_head = out_grad[:, low:high].reshape(row_count, group_size, HD)
        key_head = kv_pair[:, head_index * HD : (head_index + 1) * HD]
        value_head = kv_pair[:, kv_width + head_index * HD : kv_width + (head_index + 1) * HD]
        scores = (
            jnp.einsum("rgd,td->rgt", query_head, key_head, preferred_element_type=jnp.float32)
            * scaling
        )
        scores = jnp.where(allowed[:, None, :], scores, -1e30)
        row_max = jnp.max(scores, axis=-1, keepdims=True)
        exp_scores = jnp.exp(scores - row_max)
        probs = exp_scores / jnp.sum(exp_scores, axis=-1, keepdims=True)
        prob_grad = jnp.einsum(
            "rgd,td->rgt", grad_head, value_head, preferred_element_type=jnp.float32
        )
        row_delta = jnp.sum(probs * prob_grad, axis=-1, keepdims=True)
        score_grad = (probs * (prob_grad - row_delta)).astype(jnp.bfloat16)
        probs_b = probs.astype(jnp.bfloat16)
        dq_head = (
            jnp.einsum("rgt,td->rgd", score_grad, key_head, preferred_element_type=jnp.float32)
            * scaling
        )
        dq_parts.append(dq_head.reshape(row_count, group_size * HD).astype(jnp.bfloat16))
        key_parts.append(
            jnp.einsum("rgt,rgd->td", score_grad, query_head, preferred_element_type=jnp.float32)
            * scaling
        )
        value_parts.append(
            jnp.einsum("rgt,rgd->td", probs_b, grad_head, preferred_element_type=jnp.float32)
        )
    query_grad = jnp.concatenate(dq_parts, axis=1)
    kv_term = jnp.concatenate(key_parts + value_parts, axis=1)
    kv_grad = lax.psum(kv_term, "vis").astype(jnp.bfloat16)
    vision_grad = jnp.einsum(
        "tc,fc->tf", kv_grad, weight_full, preferred_element_type=jnp.float32
    ).astype(jnp.bfloat16)
    weight_term = jnp.einsum("tf,tc->fc", images, kv_grad, preferred_element_type=jnp.float32)
    weight_grad = lax.psum_scatter(
        weight_term.astype(jnp.bfloat16), "txt", scatter_dimension=1, tiled=True
    ).astype(jnp.float32)
    return (query_grad, vision_grad[None], weight_grad)


def solution(mesh):
    in_specs = (
        P(("txt", "vis"), None),
        P(("txt", "vis"), None),
        P("txt", None, "vis"),
        P("vis", "txt"),
        P("txt", None, None),
        P("txt"),
    )
    out_specs = (P(("txt", "vis"), None), P("txt", None, "vis"), P("vis", "txt"))
    return jax.shard_map(local, mesh=mesh, in_specs=in_specs, out_specs=out_specs, check_vma=False)
```

profile of v0, /device:TPU:4, one launch (start us, length us, event | category | flops | bytes accessed | tf_op | source)
XLA Modules:
  0.0 642.1 jit_solution(8331430664990680190)
XLA Ops:
  9.4 25.0 %all_gather.3 = bf16[128,1024]{1,0:T(8,128)(2,1)S(1)} all-gather(bf16[128,128]{1,0:T(8,128)(2,1)} %param.9), channel_id=1, replica_groups=mesh['vis'=64,'txt'=8] {'txt'}, dimensions={1}, use_global_device_ids=true | all-gather | bytes 294912 | tf_op jit(solution)/shard_map/all_gather | solution.py:18
  34.4 1.3 fusion.69
  37.2 0.9 copy.147
  38.0 0.9 copy.151
  39.7 0.8 copy.153
  40.9 256.6 %all-reduce.2 = bf16[384,1024]{1,0:T(8,128)(2,1)S(1)} all-reduce(f32[384,1024]{1,0:T(8,128)S(1)} %fusion.53), channel_id=1, replica_groups=mesh['vis'=64,'txt'=8] {'vis'}, use_global_device_ids=true, to_apply=%region_0.0 | all-reduce | flops 393216 | bytes 2359296 | tf_op jit(solution)/shard_map/psum | solution.py:22
  297.7 1.2 fusion.71
  298.9 2.3 fusion.72
  301.3 2.3 fusion.73
  303.6 1.8 fusion.74
  305.4 1.9 fusion.17
  307.3 1.0 fusion.19
  308.3 1.0 fusion.40
  309.8 1.8 fusion.10
  312.3 1.1 copy-done.4
  314.7 1.1 fusion.38
  315.8 1.1 fusion.36
  316.9 1.1 fusion.34
  317.9 2.7 fusion.32
  320.6 2.7 fusion.31
  323.4 2.6 fusion.30
  325.9 2.6 fusion.29
  328.6 261.5 %all-reduce.3 = bf16[384,1024]{0,1:T(8,128)(2,1)S(1)} all-reduce(f32[384,1024]{0,1:T(8,128)} %fusion.29), channel_id=1, replica_groups=mesh['vis'=64,'txt'=8] {'vis'}, use_global_device_ids=true, to_apply=%region_13.14 | all-reduce | flops 393216 | bytes 2359296 | tf_op jit(solution)/shard_map/psum | solution.py:67
  590.1 1.1 fusion.28
  591.2 2.0 fusion.27
  593.2 1.2 fusion.26
  594.5 1.3 fusion.25
  595.8 1.2 fusion.24
  597.0 1.1 fusion.41
  598.7 1.0 pad_maximum_fusion
  599.7 34.0 %reduce-scatter.2.cloned.1.call-done = bf16[128,128]{0,1:T(8,128)(2,1)} async-done(((bf16[128,1024]{0,1:T(8,128)(2,1)}), bf16[128,128]{0,1:T(8,128)(2,1)}) %reduce-scatter.2.cloned.1.call-update) | async-done | bytes 32784 | tf_op jit(solution)/shard_map/reduce_scatter | solution.py:72
  633.8 1.5 copy.117
  (84 shorter events, 7.3 us)
Async XLA Ops:
  7.2 33.4 %copy-start = (bf16[1,384,128]{2,1,0:T(8,128)(2,1)S(1)}, bf16[1,384,128]{2,1,0:T(8,128)(2,1)}, u32[]{:S(2)}) copy-start(bf16[1,384,128]{2,1,0:T(8,128)(2,1)} %param.8) | copy-start | bytes 294916
  7.2 626.6 %reduce-scatter.2.cloned.1.call-start = ((), (), s32[]{:S(2)}) async-start(), calls=%async_computation.1 | async-start | bytes 294912 | tf_op jit(solution)/shard_map/reduce_scatter | solution.py:72
  35.7 1.4 copy-start.18
  36.7 262.2 %copy-start.8 = (bf16[128,1024]{0,1:T(8,128)(2,1)}, bf16[128,1024]{0,1:T(8,128)(2,1)S(1)}, u32[]{:S(2)}) copy-start(bf16[128,1024]{0,1:T(8,128)(2,1)S(1)} %copy.150) | copy-start | bytes 786436
  36.9 264.4 %copy-start.14 = (bf16[128,1024]{0,1:T(8,128)(2,1)}, bf16[128,1024]{0,1:T(8,128)(2,1)S(1)}, u32[]{:S(2)}) copy-start(bf16[128,1024]{0,1:T(8,128)(2,1)S(1)} %copy.148) | copy-start | bytes 786436
  37.1 260.6 %copy-start.11 = (bf16[128,1024]{0,1:T(8,128)(2,1)}, bf16[128,1024]{0,1:T(8,128)(2,1)S(1)}, u32[]{:S(2)}) copy-start(bf16[128,1024]{0,1:T(8,128)(2,1)S(1)} %copy.152) | copy-start | bytes 786436
  297.6 14.7 %copy-start.3 = (bf16[384,1024]{1,0:T(8,128)(2,1)}, bf16[384,1024]{1,0:T(8,128)(2,1)S(1)}, u32[]{:S(2)}) copy-start(bf16[384,1024]{1,0:T(8,128)(2,1)S(1)} %all-reduce.2) | copy-start | bytes 2359300
  298.9 10.4 %copy-start.6 = (f32[128,8,384]{0,2,1:T(8,128)}, f32[128,8,384]{0,2,1:T(8,128)S(1)}, u32[]{:S(2)}) copy-start(f32[128,8,384]{0,2,1:T(8,128)S(1)} %get-tuple-element.21) | copy-start | bytes 4718596
  301.3 2.3 copy-start.16
  303.6 1.8 copy-start.24
  305.4 1.9 copy-start.28
  305.4 1.9 copy-start.7
  307.3 1.0 copy-start.17
  307.3 2.0 copy-start.22
  307.3 2.0 copy-start.25
  309.7 1.9 copy-start.5
  309.7 1.9 copy-start.20
  309.7 1.9 copy-start.26
  312.0 1.4 copy-start.4
  312.0 1.4 copy-start.23
  312.0 1.4 copy-start.27
  313.8 1.0 copy-start.15
  313.8 2.0 copy-start.9
  314.7 3.2 copy-start.1
  314.7 2.1 copy-start.12
  320.6 2.7 copy-start.10
  320.6 2.7 copy-start.21
  323.4 2.6 copy-start.13
  591.2 3.3 copy-start.2
  594.5 3.6 copy-start.19
Sparse Core Ops, SparseCore 0:
  591.3 42.4 reduce-scatter.1
where the time goes:
time: 643 us; the launch traced here: 642 us
  blocking collectives  543 us (84%)
  waiting for transfers between devices  34.1 us (5%)
  matrix products  33.8 us (5%)
  between operations  15.1 us (2%)
  local copies, waits for them, and re-layouts  11.7 us (2%)
    psum x1, blocking collectives, local(): kv_grad = lax.psum(kv_term, 'vis').astype(jnp.bfloat16)  261 us
    psum x1, blocking collectives, local(): kv_pair = lax.psum(partial_value, 'vis').astype(jnp.bfloat16)  257 us
    reduce_scatter x1, waiting for transfers between devices, local(): lax.psum_scatter(weight_term.astype(jnp.bfloat16), 'txt', scatter_dimensi...  34 us
    all_gather x1, blocking collectives, local(): weight_full = lax.all_gather(w_kv, 'txt', axis=1, tiled=True)  25 us
  transfers between devices with their start and end apart: 1, of which 1 were waited for; matrix products, arithmetic and copies ran while one was open for 1% of the time, Pallas kernels for 0%

commit v1 on v0

v1 whole, which is shorter than its diff:
```python
import jax
import jax.numpy as jnp
from jax import lax
from jax.experimental import pallas as pl
from jax.experimental.pallas import tpu as pltpu
from jax.sharding import PartitionSpec as P

HD = 128
QH = 32
KVH = 4
GROUP = QH // KVH
IMG_DOC = 16
IMG_LEN = 24
TOK = IMG_DOC * IMG_LEN
NZ, NX, NY = 8, 4, 8
PIECE = TOK // NZ
SCALE = HD ** (-0.5)
LOG2E = 1.4426950408889634
MESH = pl.DeviceIdType.MESH
F32, BF16 = jnp.float32, jnp.bfloat16

CORE, XS, ZS, AZ, AX, AC = 0, 4, 8, 16, 24, 28
FWD, BWD, WG, YS = 0, 32, 64, 72
SEMS = 80


def near_first(n):
    return sorted(range(1, n), key=lambda k: min(k, n - k))


def far_first(n):
    return near_first(n)[::-1]


def body(
    q_hbm, do_hbm, vision_ref, w_ref, links_ref, count_ref,
    dq_hbm, vg_ref, wg_ref,
    q_ref, do_ref, dq_ref, bias_ref, vt_ref, kt_ref, w_all,
    p_ref, sg_ref, grads,
    own1, csend1, crecv1, xsend1, xrecv1, xown1, zsend1, zrecv1, kv1,
    own2, csend2, crecv2, xsend2, xrecv2, xown2, zsend2, zrecv2, kv2,
    ysend, yrecv, yown,
    ssem, rsem, lsem,
):
    v = lax.axis_index("vis")
    t = lax.axis_index("txt")
    core = lax.rem(v, 2)
    x = lax.rem(lax.div(v, 2), NX)
    z = lax.div(v, 2 * NX)
    other = 1 - core
    mine = core * KVH + x

    def vis_at(zz, xx, cc):
        return (zz * NX + xx) * 2 + cc

    partner = (vis_at(z, x, other), t)

    def x_dev(k):
        return (vis_at(z, lax.rem(x + k, NX), core), t)

    def z_dev(k):
        return (vis_at(lax.rem(z + k, NZ), x, core), t)

    def y_dev(k):
        return (v, lax.rem(t + k, NY))

    def piece(zz):
        return pl.ds(pl.multiple_of(zz * PIECE, PIECE), PIECE)

    def link(src, dst, sem, dev):
        return pltpu.make_async_remote_copy(
            src_ref=src, dst_ref=dst, send_sem=ssem.at[sem], recv_sem=rsem.at[sem],
            device_id=dev, device_id_type=MESH,
        )

    q_in = pltpu.make_async_copy(q_hbm, q_ref, lsem.at[0])
    do_in = pltpu.make_async_copy(do_hbm, do_ref, lsem.at[1])
    q_in.start()
    do_in.start()

    barrier = pltpu.get_barrier_semaphore()
    partners = (
        [partner]
        + [x_dev(k) for k in range(1, NX)]
        + [z_dev(k) for k in range(1, NZ)]
        + [y_dev(k) for k in range(1, NY)]
    )
    for dev in partners:
        pl.semaphore_signal(barrier, inc=1, device_id=dev, device_id_type=MESH)
    pl.semaphore_wait(barrier, len(partners))

    def w_copy(k):
        return link(w_ref, w_all.at[t], WG + k, y_dev(k))

    for k in far_first(NY):
        w_copy(k).start()
    w_all[t] = w_ref[...]

    block = lax.broadcasted_iota(jnp.int32, links_ref.shape[1:], 1)
    slot = lax.broadcasted_iota(jnp.int32, (IMG_DOC, 1), 0)
    linked = jnp.sum(jnp.where(block == v, links_ref[0], 0), axis=1, keepdims=True)
    bias = jnp.where((linked == 1) & (slot < count_ref[0]), 0.0, -1e30)
    for s in range(IMG_DOC):
        bias_ref[s * IMG_LEN : (s + 1) * IMG_LEN, :] = jnp.broadcast_to(
            bias[s : s + 1, :], (IMG_LEN, HD)
        )
    vt_ref[...] = vision_ref[0].T

    class Sums:
        def __init__(self, base, own, csend, crecv, xsend, xrecv, xown, zsend, zrecv, kv):
            self.base, self.own, self.csend, self.crecv = base, own, csend, crecv
            self.xsend, self.xrecv, self.xown = xsend, xrecv, xown
            self.zsend, self.zrecv, self.kv = zsend, zrecv, kv

        def core_copy(self, h):
            return link(self.csend.at[h], self.crecv.at[h], self.base + CORE + h, partner)

        def x_copy(self, k):
            return link(self.xsend.at[k], self.xrecv.at[k], self.base + XS + k, x_dev(k))

        def z_copy(self, k):
            rows = piece(lax.rem(z + k, NZ))
            return link(self.zsend.at[rows, :], self.zrecv.at[k], self.base + ZS + k, z_dev(k))

        def az_copy(self, k, zz):
            ref = self.kv.at[mine, piece(zz), :]
            return link(ref, ref, self.base + AZ + k, z_dev(k))

        def ax_copy(self, k, h):
            ref = self.kv.at[core * KVH + h]
            return link(ref, ref, self.base + AX + k, x_dev(k))

        def ac_copy(self, kind, h):
            ref = self.kv.at[kind * KVH + h]
            return link(ref, ref, self.base + AC + h, partner)

        def x_step(self, h):
            self.core_copy(h).wait_recv()
            total = self.own[h] + self.crecv[h].astype(F32)
            k = lax.rem(h - x + NX, NX)

            @pl.when(k == 0)
            def _():
                self.xown[...] = total

            @pl.when(k != 0)
            def _():
                self.xsend[k] = total.astype(BF16)
                self.x_copy(k).start()

        def z_stage(self):
            total = self.xown[...]
            for k in near_first(NX):
                self.x_copy(k).wait_recv()
                total = total + self.xrecv[k].astype(F32)
            self.xown[...] = total
            self.zsend[...] = total.astype(BF16)
            for k in far_first(NZ):
                self.z_copy(k).start()
            part = self.xown[piece(z), :]
            for k in near_first(NZ):
                self.z_copy(k).wait_recv()
                part = part + self.zrecv[k].astype(F32)
            self.kv[mine, piece(z), :] = part.astype(BF16)
            for k in far_first(NZ):
                self.az_copy(k, z).start()
            for k in near_first(NZ):
                self.az_copy(k, lax.rem(z - k + NZ, NZ)).wait_recv()
            self.ac_copy(core, x).start()
            for k in near_first(NX):
                self.ax_copy(k, x).start()

        def x_arrive(self, i):
            h = lax.rem(x + i, NX)
            self.ax_copy(NX - i, h).wait_recv()
            self.ac_copy(core, h).start()

        def partner_arrive(self, i):
            self.ac_copy(other, lax.rem(x + i, NX)).wait_recv()

        def sent(self):
            for h in range(KVH):
                self.core_copy(h).wait_send()
                self.ac_copy(core, h).wait_send()
            for k in range(1, NX):
                self.x_copy(k).wait_send()
                self.ax_copy(k, x).wait_send()
            for k in range(1, NZ):
                self.z_copy(k).wait_send()
                self.az_copy(k, z).wait_send()

    fwd = Sums(FWD, own1, csend1, crecv1, xsend1, xrecv1, xown1, zsend1, zrecv1, kv1)
    bwd = Sums(BWD, own2, csend2, crecv2, xsend2, xrecv2, xown2, zsend2, zrecv2, kv2)

    def w_loop(n, carry):
        near = lax.div(n + 1, 2)
        j = jnp.where(lax.rem(n, 2) == 1, near, lax.rem(NY - near, NY))

        @pl.when(n < NY)
        def _():
            b = lax.rem(t + j, NY)

            @pl.when(j != 0)
            def _():
                k = NY - j
                link(w_ref, w_all.at[b], WG + k, y_dev(k)).wait_recv()

            part = jnp.dot(vision_ref[0], w_all[b], preferred_element_type=F32)
            h = lax.rem(b, KVH)
            kind = lax.div(b, KVH)

            @pl.when(kind == core)
            def _():
                fwd.own[h] = part

            @pl.when(kind != core)
            def _():
                fwd.csend[h] = part.astype(BF16)
                fwd.core_copy(h).start()

        @pl.when(n >= NY - 2)
        def _():
            j = jnp.where(n < NY, n - (NY - 4), NY + 1 - n)
            fwd.x_step(lax.rem(t + j, KVH))

        return carry

    lax.fori_loop(0, NY + 2, w_loop, 0)
    fwd.z_stage()

    q_in.wait()
    do_in.wait()

    def turn(n):
        return jnp.where(n < 2, 1 + 2 * n, 6 - 2 * n)

    def out_copy(i):
        h = lax.rem(x + i, NX)
        span = pl.ds(pl.multiple_of(h * GROUP * HD, GROUP * HD), GROUP * HD)
        return pltpu.make_async_copy(dq_ref.at[:, span], dq_hbm.at[:, span], lsem.at[2 + i])

    def attend(n, carry):
        i = turn(n)
        h = lax.rem(x + i, NX)
        base = h * GROUP * HD

        def columns(j):
            return pl.ds(pl.multiple_of(base + j * HD, HD), HD)

        fwd.partner_arrive(i)
        kt_ref[...] = kv1[h].T

        def some_heads(m, inner):
            @pl.when((m == 1) & (n == 0))
            def _():
                fwd.x_arrive(2)

            @pl.when((m == 1) & (n > 0))
            def _():
                bwd.x_step(lax.rem(x + turn(n - 1), NX))

            dims = (((1,), (1,)), ((), ()))
            for r in range(GROUP // 2):
                j = m * (GROUP // 2) + r
                place = pl.ds(pl.multiple_of(j * HD, HD), HD)
                q_j = q_ref[:, columns(j)]
                do_j = do_ref[:, columns(j)]
                s = lax.dot_general(kv1[h], q_j, dims, preferred_element_type=F32)
                g = lax.dot_general(kv1[KVH + h], do_j, dims, preferred_element_type=F32)
                s = s * (SCALE * LOG2E) + bias_ref[...]
                e = jnp.exp2(s - jnp.max(s, axis=0, keepdims=True))
                probs = e * (1.0 / jnp.sum(e, axis=0, keepdims=True))
                delta = jnp.sum(probs * g, axis=0, keepdims=True)
                p_ref[:, place] = probs.astype(BF16)
                sg_ref[:, place] = (probs * (g - delta)).astype(BF16)
            return inner

        lax.fori_loop(0, 2, some_heads, 0)
        q_rows = jnp.concatenate([q_ref[:, columns(j)] for j in range(GROUP)], axis=0)
        do_rows = jnp.concatenate([do_ref[:, columns(j)] for j in range(GROUP)], axis=0)
        grads[0] = jnp.dot(sg_ref[...], q_rows, preferred_element_type=F32) * SCALE
        grads[1] = jnp.dot(p_ref[...], do_rows, preferred_element_type=F32)
        bwd.csend[h] = grads[other].astype(BF16)
        bwd.core_copy(h).start()
        bwd.own[h] = grads[core]
        dq_t = jnp.dot(kt_ref[...], sg_ref[...], preferred_element_type=F32) * SCALE
        for j in range(GROUP):
            dq_ref[:, columns(j)] = dq_t[:, j * HD : (j + 1) * HD].T.astype(BF16)
        out_copy(i).start()
        return carry

    fwd.x_arrive(1)
    fwd.x_arrive(3)
    lax.fori_loop(0, KVH, attend, 0)
    bwd.x_step(x)
    bwd.z_stage()

    def y_copy(k):
        return link(ysend.at[k], yrecv.at[k], YS + k, y_dev(k))

    images = xown1
    images[...] = jnp.zeros((TOK, HD), F32)

    def y_loop(n, carry):
        m = lax.rem(n, KVH)
        i = jnp.where(m < 2, m, 5 - m)
        kind = jnp.where(n < KVH, core, other)
        b = kind * KVH + lax.rem(x + i, NX)

        @pl.when((n > 0) & (n < KVH))
        def _():
            bwd.x_arrive(i)

        @pl.when(n >= KVH)
        def _():
            bwd.partner_arrive(i)

        part = jnp.dot(vt_ref[...], kv2[b], preferred_element_type=F32)
        k = lax.rem(b - t + NY, NY)

        @pl.when(k == 0)
        def _():
            yown[...] = part

        @pl.when(k != 0)
        def _():
            ysend[k] = part.astype(BF16)
            y_copy(k).start()

        images[...] += lax.dot_general(
            kv2[b], w_all[b], (((1,), (1,)), ((), ())), preferred_element_type=F32
        )
        return carry

    lax.fori_loop(0, 2 * KVH, y_loop, 0)
    vg_ref[0] = images[...].astype(BF16)

    grad = yown[...]
    for k in near_first(NY):
        y_copy(k).wait_recv()
        grad = grad + yrecv[k].astype(F32)
    wg_ref[...] = grad

    for i in range(KVH):
        out_copy(i).wait()
    fwd.sent()
    bwd.sent()
    for k in range(1, NY):
        w_copy(k).wait_send()
        y_copy(k).wait_send()


def local(queries, out_grad, vision, w_kv, links, img_count):
    rows, width = queries.shape
    anywhere = pl.BlockSpec(memory_space=pl.ANY)
    vmem = pl.BlockSpec(memory_space=pltpu.VMEM)
    smem = pl.BlockSpec(memory_space=pltpu.SMEM)
    sums = [
        pltpu.VMEM((KVH, TOK, HD), F32),
        pltpu.VMEM((KVH, TOK, HD), BF16),
        pltpu.VMEM((KVH, TOK, HD), BF16),
        pltpu.VMEM((NX, TOK, HD), BF16),
        pltpu.VMEM((NX, TOK, HD), BF16),
        pltpu.VMEM((TOK, HD), F32),
        pltpu.VMEM((TOK, HD), BF16),
        pltpu.VMEM((NZ, PIECE, HD), BF16),
        pltpu.VMEM((2 * KVH, TOK, HD), BF16),
    ]
    return pl.pallas_call(
        body,
        out_shape=(
            jax.ShapeDtypeStruct(queries.shape, BF16),
            jax.ShapeDtypeStruct(vision.shape, BF16),
            jax.ShapeDtypeStruct(w_kv.shape, F32),
        ),
        in_specs=[anywhere, anywhere, vmem, vmem, vmem, smem],
        out_specs=(anywhere, vmem, vmem),
        scratch_shapes=[
            pltpu.VMEM((rows, width), BF16),
            pltpu.VMEM((rows, width), BF16),
            pltpu.VMEM((rows, width), BF16),
            pltpu.VMEM((TOK, HD), F32),
            pltpu.VMEM((HD, TOK), BF16),
            pltpu.VMEM((HD, TOK), BF16),
            pltpu.VMEM((NY, HD, HD), BF16),
            pltpu.VMEM((TOK, GROUP * HD), BF16),
            pltpu.VMEM((TOK, GROUP * HD), BF16),
            pltpu.VMEM((2, TOK, HD), F32),
            *sums,
            *sums,
            pltpu.VMEM((NY, HD, HD), BF16),
            pltpu.VMEM((NY, HD, HD), BF16),
            pltpu.VMEM((HD, HD), F32),
            pltpu.SemaphoreType.DMA((SEMS,)),
            pltpu.SemaphoreType.DMA((SEMS,)),
            pltpu.SemaphoreType.DMA((6,)),
        ],
        compiler_params=pltpu.CompilerParams(
            collective_id=0, has_side_effects=True, vmem_limit_bytes=40 * 1024 * 1024
        ),
    )(queries, out_grad, vision, w_kv, jnp.swapaxes(links, 1, 2), img_count)


def solution(mesh):
    in_specs = (
        P(("txt", "vis"), None),
        P(("txt", "vis"), None),
        P("txt", None, "vis"),
        P("vis", "txt"),
        P("txt", None, None),
        P("txt"),
    )
    out_specs = (P(("txt", "vis"), None), P("txt", None, "vis"), P("vis", "txt"))
    return jax.shard_map(local, mesh=mesh, in_specs=in_specs, out_specs=out_specs, check_vma=False)
```

time: 643 us -> 92.4 us (0.14)
  the two profiles are of different devices: /device:TPU:4 before, /device:TPU:17 now
where the time goes in v1:
time: 92.4 us; the launch traced here: 92 us
  Pallas kernels  83.7 us (91%)
  local copies, waits for them, and re-layouts  7.03 us (8%)
  between operations  1.3 us (1%)
    pallas_call x1, Pallas kernels, local(): pl.pallas_call(body, out_shape=(jax.ShapeDtypeStruct(queries.shape, BF16)...  83.7 us
    unnamed x13, local copies, waits for them, and re-layouts  7.03 us

profile of v1, /device:TPU:17, one launch (start us, length us, event | category | flops | bytes accessed | tf_op | source)
XLA Modules:
  0.0 92.0 jit_solution(6026305700039247143)
XLA Ops:
  1.3 0.0 copy-start
  1.3 1.2 %copy-done = bf16[128,4096]{1,0:T(8,128)(2,1)S(1)} copy-done((bf16[128,4096]{1,0:T(8,128)(2,1)S(1)}, bf16[128,4096]{1,0:T(8,128)(2,1)}, u32[]{:S(2)}) %copy-start) | copy-done | bytes 1048600
  2.5 0.0 copy-start.1
  2.5 1.2 %copy-done.1 = bf16[128,4096]{1,0:T(8,128)(2,1)S(1)} copy-done((bf16[128,4096]{1,0:T(8,128)(2,1)S(1)}, bf16[128,4096]{1,0:T(8,128)(2,1)}, u32[]{:S(2)}) %copy-start.1) | copy-done | bytes 1048600
  3.7 0.0 copy-start.2
  3.7 0.9 copy-done.2
  4.6 0.0 copy-start.3
  4.6 0.8 copy-done.3
  5.4 0.0 copy-start.4
  5.4 0.7 copy-done.4
  6.1 83.7 %shard_map.85 = (bf16[128,4096]{1,0:T(8,128)(2,1)S(1)}, bf16[1,384,128]{2,1,0:T(8,128)(2,1)S(1)}, f32[128,128]{1,0:T(8,128)S(1)}) custom-call(bf16[128,4096]{1,0:T(8,128)(2,1)S(1)} %copy-done, bf16[128,4096]{1,0:T(8,128)(2,1)S(1)} %copy-done.1, bf16[1,384,128]{2,1,0:T(8,128)(2,1)S(1)} %copy-done.2, bf16[128,128]{1,0:T(8,128)(2,1)S(1)} %copy-done.3, ...), custom_call_target="tpu_custom_call" | custom-call | tf_op jit(solution)/shard_map/pallas_call | solution.py:369
  89.8 1.0 %copy.13 = bf16[128,4096]{1,0:T(8,128)(2,1)} copy(bf16[128,4096]{1,0:T(8,128)(2,1)S(1)} %get-tuple-element.6) | data formatting | bytes 2097152
  90.8 0.6 copy.14
  91.4 0.6 copy.15
Async XLA Ops:
  1.3 1.2 %copy-start = (bf16[128,4096]{1,0:T(8,128)(2,1)S(1)}, bf16[128,4096]{1,0:T(8,128)(2,1)}, u32[]{:S(2)}) copy-start(bf16[128,4096]{1,0:T(8,128)(2,1)} %q_hbm.1) | copy-start | bytes 3145732
  2.5 1.2 %copy-start.1 = (bf16[128,4096]{1,0:T(8,128)(2,1)S(1)}, bf16[128,4096]{1,0:T(8,128)(2,1)}, u32[]{:S(2)}) copy-start(bf16[128,4096]{1,0:T(8,128)(2,1)} %do_hbm.1) | copy-start | bytes 3145732
  3.7 0.9 copy-start.2
  4.6 0.8 copy-start.3
  5.4 0.7 copy-start.4

commit v2 on v1

v2 whole, which is shorter than its diff:
```python
import jax
import jax.numpy as jnp
from jax import lax
from jax.experimental import pallas as pl
from jax.experimental.pallas import tpu as pltpu
from jax.sharding import PartitionSpec as P

HD = 128
QH = 32
KVH = 4
GROUP = QH // KVH
IMG_DOC = 16
IMG_LEN = 24
TOK = IMG_DOC * IMG_LEN
NZ, NX, NY = 8, 4, 8
PIECE = TOK // NZ
SCALE = HD ** (-0.5)
LOG2E = 1.4426950408889634
MESH = pl.DeviceIdType.MESH
F32, BF16 = jnp.float32, jnp.bfloat16

CORE, XS, ZS, AZ, AX, AC = 0, 4, 8, 16, 24, 28
FWD, BWD, WG, YS = 0, 32, 64, 74
SEMS = 82


def near_first(n):
    return sorted(range(1, n), key=lambda k: min(k, n - k))


def far_first(n):
    return near_first(n)[::-1]


def body(
    q_hbm, do_hbm, vision_hbm, w_hbm, links_hbm, count_hbm,
    dq_hbm, vg_ref, wg_ref,
    q_ref, do_ref, dq_ref, vision_ref, links_ref, count_ref, bias_ref, vt_ref, w_all,
    p_ref, sg_ref, grads, images,
    own1, csend1, crecv1, xsend1, xrecv1, xown1, zsend1, zrecv1, kv1,
    csend2, crecv2, xsend2, xrecv2, xown2, zsend2, zrecv2, kv2,
    ysend, yrecv, yown,
    ssem, rsem, lsem,
):
    v = lax.axis_index("vis")
    t = lax.axis_index("txt")
    core = lax.rem(v, 2)
    x = lax.rem(lax.div(v, 2), NX)
    z = lax.div(v, 2 * NX)
    other = 1 - core
    mine = core * KVH + x

    def vis_at(zz, xx, cc):
        return (zz * NX + xx) * 2 + cc

    partner = (vis_at(z, x, other), t)

    def x_dev(k):
        return (vis_at(z, lax.rem(x + k, NX), core), t)

    def z_dev(k):
        return (vis_at(lax.rem(z + k, NZ), x, core), t)

    def y_dev(k):
        return (v, lax.rem(t + k, NY))

    def piece(zz):
        return pl.ds(pl.multiple_of(zz * PIECE, PIECE), PIECE)

    def link(src, dst, sem, dev):
        return pltpu.make_async_remote_copy(
            src_ref=src, dst_ref=dst, send_sem=ssem.at[sem], recv_sem=rsem.at[sem],
            device_id=dev, device_id_type=MESH,
        )

    fetches = [
        pltpu.make_async_copy(src, dst, lsem.at[n])
        for n, (src, dst) in enumerate([
            (w_hbm, w_all.at[t]), (vision_hbm, vision_ref), (links_hbm, links_ref),
            (count_hbm, count_ref), (q_hbm, q_ref), (do_hbm, do_ref),
        ])
    ]
    for fetch in fetches:
        fetch.start()

    barrier = pltpu.get_barrier_semaphore()
    partners = (
        [partner]
        + [x_dev(k) for k in range(1, NX)]
        + [z_dev(k) for k in range(1, NZ)]
        + [y_dev(k) for k in range(1, NY)]
    )
    for dev in partners:
        pl.semaphore_signal(barrier, inc=1, device_id=dev, device_id_type=MESH)
    pl.semaphore_wait(barrier, len(partners))

    def w_copy(k):
        return link(w_hbm, w_all.at[t], WG + NY - k, y_dev(k))

    def w_third(j):
        b = lax.rem(t + j, NY)
        up = j == 2
        return link(w_all.at[b], w_all.at[b], WG + (3 if up else 5), y_dev(NY - 1 if up else 1))

    def w_fourth(j):
        b = lax.rem(t + j, NY)
        up = j == 2
        half = w_all.at[b, pl.ds(0 if up else HD // 2, HD // 2), :]
        return link(half, half, WG + (4 if up else 8), y_dev(NY - 2 if up else 2))

    near_w = (1, NY - 1, 2, NY - 2)
    for k in near_w:
        w_copy(k).start()
    for fetch in fetches[:4]:
        fetch.wait()

    block = lax.broadcasted_iota(jnp.int32, links_ref.shape[1:], 1)
    slot = lax.broadcasted_iota(jnp.int32, (IMG_DOC, 1), 0)
    linked = jnp.sum(jnp.where(block == v, links_ref[0], 0), axis=1, keepdims=True)
    bias = jnp.where((linked == 1) & (slot < count_ref[0]), 0.0, -1e30)
    for s in range(IMG_DOC):
        bias_ref[s * IMG_LEN : (s + 1) * IMG_LEN, :] = jnp.broadcast_to(
            bias[s : s + 1, :], (IMG_LEN, HD)
        )
    vt_ref[...] = vision_ref[0].T

    class Sums:
        def __init__(self, base, own_at, csend, crecv, xsend, xrecv, xown, zsend, zrecv, kv):
            self.base, self.own_at, self.csend, self.crecv = base, own_at, csend, crecv
            self.xsend, self.xrecv, self.xown = xsend, xrecv, xown
            self.zsend, self.zrecv, self.kv = zsend, zrecv, kv

        def core_copy(self, h):
            return link(self.csend.at[h], self.crecv.at[h], self.base + CORE + h, partner)

        def x_copy(self, k):
            return link(self.xsend.at[k], self.xrecv.at[k], self.base + XS + k, x_dev(k))

        def z_copy(self, k):
            rows = piece(lax.rem(z + k, NZ))
            return link(self.zsend.at[rows, :], self.zrecv.at[k], self.base + ZS + k, z_dev(k))

        def az_copy(self, k, zz):
            ref = self.kv.at[mine, piece(zz), :]
            return link(ref, ref, self.base + AZ + k, z_dev(k))

        def ax_copy(self, k, h):
            ref = self.kv.at[core * KVH + h]
            return link(ref, ref, self.base + AX + k, x_dev(k))

        def ac_copy(self, kind, h):
            ref = self.kv.at[kind * KVH + h]
            return link(ref, ref, self.base + AC + h, partner)

        def x_step(self, h):
            self.core_copy(h).wait_recv()
            total = self.own_at(h) + self.crecv[h].astype(F32)
            k = lax.rem(h - x + NX, NX)

            @pl.when(k == 0)
            def _():
                self.xown[...] = total

            @pl.when(k != 0)
            def _():
                self.xsend[k] = total.astype(BF16)
                self.x_copy(k).start()

        def z_stage(self, first=lambda: None, second=lambda: None):
            total = self.xown[...]
            for k in near_first(NX):
                self.x_copy(k).wait_recv()
                total = total + self.xrecv[k].astype(F32)
            self.xown[...] = total
            self.zsend[...] = total.astype(BF16)
            for k in far_first(NZ):
                self.z_copy(k).start()
            first()
            part = self.xown[piece(z), :]
            for k in near_first(NZ):
                self.z_copy(k).wait_recv()
                part = part + self.zrecv[k].astype(F32)
            self.kv[mine, piece(z), :] = part.astype(BF16)
            for k in far_first(NZ):
                self.az_copy(k, z).start()
            second()
            for k in near_first(NZ):
                self.az_copy(k, lax.rem(z - k + NZ, NZ)).wait_recv()
            self.ac_copy(core, x).start()
            for k in near_first(NX):
                self.ax_copy(k, x).start()

        def x_arrive(self, i):
            h = lax.rem(x + i, NX)
            self.ax_copy(NX - i, h).wait_recv()
            self.ac_copy(core, h).start()

        def partner_arrive(self, i):
            self.ac_copy(other, lax.rem(x + i, NX)).wait_recv()

        def sent(self):
            for h in range(KVH):
                self.core_copy(h).wait_send()
                self.ac_copy(core, h).wait_send()
            for k in range(1, NX):
                self.x_copy(k).wait_send()
                self.ax_copy(k, x).wait_send()
            for k in range(1, NZ):
                self.z_copy(k).wait_send()
                self.az_copy(k, z).wait_send()

    fwd = Sums(FWD, lambda h: own1[h], csend1, crecv1, xsend1, xrecv1, xown1, zsend1, zrecv1, kv1)
    bwd = Sums(BWD, lambda h: grads[h, core], csend2, crecv2, xsend2, xrecv2, xown2, zsend2, zrecv2, kv2)

    def near(n):
        far = lax.div(n + 1, 2)
        return jnp.where(lax.rem(n, 2) == 1, far, lax.rem(NY - far, NY))

    def w_loop(n, carry):
        @pl.when(n < NY)
        def _():
            j = near(n)
            b = lax.rem(t + j, NY)

            @pl.when((j != 0) & (j != 4))
            def _():
                link(w_hbm, w_all.at[b], WG + j, y_dev(1)).wait_recv()

            for hop in (2, 6):
                @pl.when(j == hop)
                def _():
                    w_third(hop).start()
                    w_fourth(hop).start()

            @pl.when(j == 4)
            def _():
                for place, low in ((4, 0), (8, HD // 2)):
                    half = w_all.at[b, pl.ds(low, HD // 2), :]
                    link(half, half, WG + place, y_dev(2)).wait_recv()

            part = jnp.dot(vision_ref[0], w_all[b], preferred_element_type=F32)
            h = lax.rem(b, KVH)
            kind = lax.div(b, KVH)

            @pl.when(kind == core)
            def _():
                own1[h] = part

            @pl.when(kind != core)
            def _():
                fwd.csend[h] = part.astype(BF16)
                fwd.core_copy(h).start()

        past = lax.rem(t + near(jnp.maximum(n - 2, 0)), NY)

        @pl.when((n >= 2) & (lax.div(past, KVH) == core))
        def _():
            fwd.x_step(lax.rem(past, KVH))

        return carry

    lax.fori_loop(0, NY + 2, w_loop, 0)
    fwd.z_stage()

    for fetch in fetches[4:]:
        fetch.wait()

    HALF = GROUP // 2

    def attend(u, carry):
        mine_now = (u == 0) | (u == 2 * KVH - 1)
        i = jnp.where(mine_now, 0, jnp.where(u >= 5, 2, jnp.where(u >= 3, 3, 1)))
        half = jnp.where(mine_now, lax.div(u, 2 * KVH - 1), lax.rem(u + 1, 2))
        h = lax.rem(x + i, NX)
        base = h * GROUP * HD + half * HALF * HD

        def columns(j):
            return pl.ds(pl.multiple_of(base + j * HD, HD), HD)

        @pl.when(u == 1)
        def _():
            fwd.x_arrive(1)

        @pl.when(half == 0)
        def _():
            fwd.partner_arrive(i)

        q = [q_ref[:, columns(j)] for j in range(HALF)]
        do = [do_ref[:, columns(j)] for j in range(HALF)]
        dims = (((1,), (1,)), ((), ()))
        bias = jnp.concatenate([bias_ref[...]] * 2, axis=1)
        for j in range(0, HALF, 2):
            two_q = jnp.concatenate(q[j : j + 2], axis=0)
            two_do = jnp.concatenate(do[j : j + 2], axis=0)
            s = lax.dot_general(kv1[h], two_q, dims, preferred_element_type=F32)
            g = lax.dot_general(kv1[KVH + h], two_do, dims, preferred_element_type=F32)
            s = s * (SCALE * LOG2E) + bias
            e = jnp.exp2(s - jnp.max(s, axis=0, keepdims=True))
            probs = e * (1.0 / jnp.sum(e, axis=0, keepdims=True))
            delta = jnp.sum(probs * g, axis=0, keepdims=True)
            p_ref[:, j * HD : (j + 2) * HD] = probs.astype(BF16)
            place = pl.ds(pl.multiple_of((half * HALF + j) * HD, HD), 2 * HD)
            sg_ref[h, :, place] = (probs * (g - delta)).astype(BF16)

        @pl.when(u == 1)
        def _():
            fwd.x_arrive(3)

        @pl.when(u == 3)
        def _():
            fwd.x_arrive(2)

        for when, done in ((4, 1), (6, 3), (7, 2)):
            @pl.when(u == when)
            def _():
                bwd.x_step(lax.rem(x + done, NX))

        place = pl.ds(pl.multiple_of(half * HALF * HD, HALF * HD), HALF * HD)
        key_part = jnp.dot(
            sg_ref[h, :, place], jnp.concatenate(q, axis=0), preferred_element_type=F32
        ) * SCALE
        value_part = jnp.dot(
            p_ref[...], jnp.concatenate(do, axis=0), preferred_element_type=F32
        )

        @pl.when(half == 0)
        def _():
            grads[h, 0] = key_part
            grads[h, 1] = value_part

        @pl.when(half == 1)
        def _():
            grads[h, 0] += key_part
            grads[h, 1] += value_part
            bwd.csend[h] = grads[h, other].astype(BF16)
            bwd.core_copy(h).start()

        return carry

    lax.fori_loop(0, 2 * KVH, attend, 0)

    def dq_copy(i):
        span = pl.ds(pl.multiple_of(lax.rem(x + i, NX) * GROUP * HD, GROUP * HD), GROUP * HD)
        return pltpu.make_async_copy(dq_ref.at[:, span], dq_hbm.at[:, span], lsem.at[6 + i])

    def query_grads(low, high):
        def one(i, carry):
            h = lax.rem(x + i, NX)
            dq = jnp.dot(kv1[h].T, sg_ref[h], preferred_element_type=F32) * SCALE
            for j in range(GROUP):
                place = pl.ds(pl.multiple_of((h * GROUP + j) * HD, HD), HD)
                dq_ref[:, place] = dq[:, j * HD : (j + 1) * HD].T.astype(BF16)
            dq_copy(i).start()
            return carry

        lax.fori_loop(low, high, one, 0)

    query_grads(0, 1)
    bwd.x_step(x)
    bwd.z_stage(lambda: query_grads(1, 3), lambda: query_grads(3, KVH))

    def y_copy(k):
        return link(ysend.at[k], yrecv.at[k], YS + k, y_dev(k))

    images[...] = jnp.zeros((TOK, HD), F32)

    def y_loop(n, carry):
        i = jnp.where(n < 2, 0, jnp.where(n >= 6, 2, 1 + 2 * lax.rem(n, 2)))
        here = (n == 0) | (n == 2) | (n == 3) | (n == 6)
        kind = jnp.where(here, core, other)
        b = kind * KVH + lax.rem(x + i, NX)

        @pl.when(here & (n > 0))
        def _():
            bwd.x_arrive(i)

        @pl.when(jnp.logical_not(here))
        def _():
            bwd.partner_arrive(i)

        part = jnp.dot(vt_ref[...], kv2[b], preferred_element_type=F32)
        k = lax.rem(b - t + NY, NY)

        @pl.when(k == 0)
        def _():
            yown[...] = part

        @pl.when(k != 0)
        def _():
            ysend[k] = part.astype(BF16)
            y_copy(k).start()

        images[...] += lax.dot_general(
            kv2[b], w_all[b], (((1,), (1,)), ((), ())), preferred_element_type=F32
        )
        return carry

    lax.fori_loop(0, 2 * KVH, y_loop, 0)
    vg_ref[0] = images[...].astype(BF16)

    grad = yown[...]
    for k in near_first(NY):
        y_copy(k).wait_recv()
        grad = grad + yrecv[k].astype(F32)
    wg_ref[...] = grad

    for i in range(KVH):
        dq_copy(i).wait()
    fwd.sent()
    bwd.sent()
    for k in near_w:
        w_copy(k).wait_send()
    for hop in (2, 6):
        w_third(hop).wait_send()
        w_fourth(hop).wait_send()
    for k in range(1, NY):
        y_copy(k).wait_send()


def write(*refs):
    sources, targets, sem = refs[:3], refs[3:6], refs[6]
    copies = [
        pltpu.make_async_copy(src, dst, sem.at[n])
        for n, (src, dst) in enumerate(zip(sources, targets))
    ]
    for copy in copies:
        copy.start()
    for copy in copies:
        copy.wait()


def local(queries, out_grad, vision, w_kv, links, img_count):
    rows, width = queries.shape
    anywhere = pl.BlockSpec(memory_space=pl.ANY)
    hbm = pl.BlockSpec(memory_space=pltpu.HBM)
    vmem = pl.BlockSpec(memory_space=pltpu.VMEM)
    sums = [
        pltpu.VMEM((KVH, TOK, HD), BF16),
        pltpu.VMEM((KVH, TOK, HD), BF16),
        pltpu.VMEM((NX, TOK, HD), BF16),
        pltpu.VMEM((NX, TOK, HD), BF16),
        pltpu.VMEM((TOK, HD), F32),
        pltpu.VMEM((TOK, HD), BF16),
        pltpu.VMEM((NZ, PIECE, HD), BF16),
        pltpu.VMEM((2 * KVH, TOK, HD), BF16),
    ]
    link_slots = jnp.swapaxes(links, 1, 2)
    out_shape = (
        jax.ShapeDtypeStruct(queries.shape, BF16),
        jax.ShapeDtypeStruct(vision.shape, BF16),
        jax.ShapeDtypeStruct(w_kv.shape, F32),
    )
    results = pl.pallas_call(
        body,
        out_shape=out_shape,
        in_specs=[hbm] * 6,
        out_specs=(hbm, vmem, vmem),
        scratch_shapes=[
            pltpu.VMEM((rows, width), BF16),
            pltpu.VMEM((rows, width), BF16),
            pltpu.VMEM((rows, width), BF16),
            pltpu.VMEM(vision.shape, BF16),
            pltpu.VMEM(link_slots.shape, jnp.int32),
            pltpu.SMEM(img_count.shape, jnp.int32),
            pltpu.VMEM((TOK, HD), F32),
            pltpu.VMEM((HD, TOK), BF16),
            pltpu.VMEM((NY, HD, HD), BF16),
            pltpu.VMEM((TOK, GROUP // 2 * HD), BF16),
            pltpu.VMEM((KVH, TOK, GROUP * HD), BF16),
            pltpu.VMEM((KVH, 2, TOK, HD), F32),
            pltpu.VMEM((TOK, HD), F32),
            pltpu.VMEM((KVH, TOK, HD), F32),
            *sums,
            *sums,
            pltpu.VMEM((NY, HD, HD), BF16),
            pltpu.VMEM((NY, HD, HD), BF16),
            pltpu.VMEM((HD, HD), F32),
            pltpu.SemaphoreType.DMA((SEMS,)),
            pltpu.SemaphoreType.DMA((SEMS,)),
            pltpu.SemaphoreType.DMA((6 + KVH,)),
        ],
        compiler_params=pltpu.CompilerParams(
            collective_id=0, has_side_effects=True, vmem_limit_bytes=60 * 1024 * 1024
        ),
    )(queries, out_grad, vision, w_kv, link_slots, img_count)
    return pl.pallas_call(
        write,
        out_shape=out_shape,
        in_specs=[anywhere] * 3,
        out_specs=(hbm,) * 3,
        scratch_shapes=[pltpu.SemaphoreType.DMA((3,))],
        compiler_params=pltpu.CompilerParams(vmem_limit_bytes=60 * 1024 * 1024),
    )(*results)


def solution(mesh):
    in_specs = (
        P(("txt", "vis"), None),
        P(("txt", "vis"), None),
        P("txt", None, "vis"),
        P("vis", "txt"),
        P("txt", None, None),
        P("txt"),
    )
    out_specs = (P(("txt", "vis"), None), P("txt", None, "vis"), P("vis", "txt"))
    return jax.shard_map(local, mesh=mesh, in_specs=in_specs, out_specs=out_specs, check_vma=False)
```

time: 92.4 us -> 121 us (1.31)
  Pallas kernels: 83.7 us -> 120 us
  local copies, waits for them, and re-layouts: 7.03 us -> 0 us
    pallas_call x1 -> x2, Pallas kernels: 83.7 us -> 120 us  [the longest x1 81.9 us: local(): pl.pallas_call(body, out_shape=out_shape, in_specs=[hbm] * 6, out_specs=(...]
    unnamed x13 -> x0, local copies, waits for them, and re-layouts: 7.03 us -> none
where the time goes in v2:
time: 121 us
  Pallas kernels  120 us (99%)
  between operations  1.29 us (1%)
    pallas_call x1, Pallas kernels, local(): pl.pallas_call(body, out_shape=out_shape, in_specs=[hbm] * 6, out_specs=(...  81.9 us
    pallas_call x1, Pallas kernels, local(): pl.pallas_call(write, out_shape=out_shape, in_specs=[anywhere] * 3, out_s...  37.9 us

profile of v2, /device:TPU:17, one launch (start us, length us, event | category | flops | bytes accessed | tf_op | source)
XLA Modules:
  0.0 121.0 jit_solution(3730883592038884095)
XLA Ops:
  1.3 81.9 %shard_map.85 = (bf16[128,4096]{1,0:T(8,128)(2,1)}, bf16[1,384,128]{2,1,0:T(8,128)(2,1)}, f32[128,128]{1,0:T(8,128)}) custom-call(bf16[128,4096]{1,0:T(8,128)(2,1)} %q_hbm.1, bf16[128,4096]{1,0:T(8,128)(2,1)} %do_hbm.1, bf16[1,384,128]{2,1,0:T(8,128)(2,1)} %vision_hbm.1, bf16[128,128]{1,0:T(8,128)(2,1)} %w_hbm.1, s32[1,16,64]{2,1,0:T(8,128)} %bitcast.1, ...), custom_call_target="tpu_custom_call" | custom-call | tf_op jit(solution)/shard_map/pallas_call | solution.py:453
  83.2 37.9 %shard_map.86 = (bf16[128,4096]{1,0:T(8,128)(2,1)}, bf16[1,384,128]{2,1,0:T(8,128)(2,1)}, f32[128,128]{1,0:T(8,128)}) custom-call(bf16[128,4096]{1,0:T(8,128)(2,1)} %get-tuple-element.6.refs_0_, bf16[1,384,128]{2,1,0:T(8,128)(2,1)} %get-tuple-element.7.refs_1_, f32[128,128]{1,0:T(8,128)} %get-tuple-element.8.refs_2_), custom_call_target="tpu_custom_call" | custom-call | tf_op jit(solution)/shard_map/pallas_call | solution.py:486

commit v3 on v2

--- a/solution.py
+++ b/solution.py
@@ -19,9 +19,9 @@
 MESH = pl.DeviceIdType.MESH
 F32, BF16 = jnp.float32, jnp.bfloat16
 
-CORE, XS, ZS, AZ, AX, AC = 0, 4, 8, 16, 24, 28
-FWD, BWD, WG, YS = 0, 32, 64, 74
-SEMS = 82
+CORE, XS, ZS, AZ, AX, AC = 0, 4, 8, 16, 24, 29
+FWD, BWD, WG, YS = 0, 33, 66, 76
+SEMS = 84
 
 
 def near_first(n):
@@ -36,7 +36,7 @@
     q_hbm, do_hbm, vision_hbm, w_hbm, links_hbm, count_hbm,
     dq_hbm, vg_ref, wg_ref,
     q_ref, do_ref, dq_ref, vision_ref, links_ref, count_ref, bias_ref, vt_ref, w_all,
-    p_ref, sg_ref, grads, images,
+    sg_ref, grads, images,
     own1, csend1, crecv1, xsend1, xrecv1, xown1, zsend1, zrecv1, kv1,
     csend2, crecv2, xsend2, xrecv2, xown2, zsend2, zrecv2, kv2,
     ysend, yrecv, yown,
@@ -117,7 +117,7 @@
     block = lax.broadcasted_iota(jnp.int32, links_ref.shape[1:], 1)
     slot = lax.broadcasted_iota(jnp.int32, (IMG_DOC, 1), 0)
     linked = jnp.sum(jnp.where(block == v, links_ref[0], 0), axis=1, keepdims=True)
-    bias = jnp.where((linked == 1) & (slot < count_ref[0]), 0.0, -1e30)
+    bias = jnp.where((linked == 1) & (slot < count_ref[...]), 0.0, -1e30)
     for s in range(IMG_DOC):
         bias_ref[s * IMG_LEN : (s + 1) * IMG_LEN, :] = jnp.broadcast_to(
             bias[s : s + 1, :], (IMG_LEN, HD)
@@ -147,6 +147,12 @@
         def ax_copy(self, k, h):
             ref = self.kv.at[core * KVH + h]
             return link(ref, ref, self.base + AX + k, x_dev(k))
+
+        def across(self, i):
+            h = lax.rem(x + i, NX)
+            up = i == 1
+            half = self.kv.at[core * KVH + h, pl.ds(0 if up else TOK // 2, TOK // 2), :]
+            return link(half, half, self.base + AX + (2 if up else 4), x_dev(3 if up else 1))
 
         def ac_copy(self, kind, h):
             ref = self.kv.at[kind * KVH + h]
@@ -187,12 +193,18 @@
             for k in near_first(NZ):
                 self.az_copy(k, lax.rem(z - k + NZ, NZ)).wait_recv()
             self.ac_copy(core, x).start()
-            for k in near_first(NX):
+            for k in (1, 3):
                 self.ax_copy(k, x).start()
 
         def x_arrive(self, i):
             h = lax.rem(x + i, NX)
-            self.ax_copy(NX - i, h).wait_recv()
+            if i == 2:
+                for place, low in ((2, 0), (4, TOK // 2)):
+                    half = self.kv.at[core * KVH + h, pl.ds(low, TOK // 2), :]
+                    link(half, half, self.base + AX + place, x_dev(1)).wait_recv()
+            else:
+                self.ax_copy(NX - i, h).wait_recv()
+                self.across(i).start()
             self.ac_copy(core, h).start()
 
         def partner_arrive(self, i):
@@ -204,7 +216,9 @@
                 self.ac_copy(core, h).wait_send()
             for k in range(1, NX):
                 self.x_copy(k).wait_send()
+            for k in (1, 3):
                 self.ax_copy(k, x).wait_send()
+                self.across(k).wait_send()
             for k in range(1, NZ):
                 self.z_copy(k).wait_send()
                 self.az_copy(k, z).wait_send()
@@ -269,7 +283,7 @@
 
     def attend(u, carry):
         mine_now = (u == 0) | (u == 2 * KVH - 1)
-        i = jnp.where(mine_now, 0, jnp.where(u >= 5, 2, jnp.where(u >= 3, 3, 1)))
+        i = jnp.where(mine_now, 0, lax.div(u + 1, 2))
         half = jnp.where(mine_now, lax.div(u, 2 * KVH - 1), lax.rem(u + 1, 2))
         h = lax.rem(x + i, NX)
         base = h * GROUP * HD + half * HALF * HD
@@ -280,48 +294,42 @@
         @pl.when(u == 1)
         def _():
             fwd.x_arrive(1)
+            fwd.x_arrive(3)
+
+        @pl.when(u == 2)
+        def _():
+            fwd.x_arrive(2)
 
         @pl.when(half == 0)
         def _():
             fwd.partner_arrive(i)
 
-        q = [q_ref[:, columns(j)] for j in range(HALF)]
-        do = [do_ref[:, columns(j)] for j in range(HALF)]
         dims = (((1,), (1,)), ((), ()))
         bias = jnp.concatenate([bias_ref[...]] * 2, axis=1)
+        key_part = value_part = None
         for j in range(0, HALF, 2):
-            two_q = jnp.concatenate(q[j : j + 2], axis=0)
-            two_do = jnp.concatenate(do[j : j + 2], axis=0)
-            s = lax.dot_general(kv1[h], two_q, dims, preferred_element_type=F32)
-            g = lax.dot_general(kv1[KVH + h], two_do, dims, preferred_element_type=F32)
+            q = jnp.concatenate([q_ref[:, columns(j)], q_ref[:, columns(j + 1)]], axis=0)
+            do = jnp.concatenate([do_ref[:, columns(j)], do_ref[:, columns(j + 1)]], axis=0)
+            s = lax.dot_general(kv1[h], q, dims, preferred_element_type=F32)
+            g = lax.dot_general(kv1[KVH + h], do, dims, preferred_element_type=F32)
             s = s * (SCALE * LOG2E) + bias
             e = jnp.exp2(s - jnp.max(s, axis=0, keepdims=True))
-            probs = e * (1.0 / jnp.sum(e, axis=0, keepdims=True))
-            delta = jnp.sum(probs * g, axis=0, keepdims=True)
-            p_ref[:, j * HD : (j + 2) * HD] = probs.astype(BF16)
+            norm = 1.0 / jnp.sum(e, axis=0, keepdims=True)
+            delta = jnp.sum(e * g, axis=0, keepdims=True) * norm
+            probs = e * norm
+            score_grad = (probs * (g - delta)).astype(BF16)
             place = pl.ds(pl.multiple_of((half * HALF + j) * HD, HD), 2 * HD)
-            sg_ref[h, :, place] = (probs * (g - delta)).astype(BF16)
-
-        @pl.when(u == 1)
-        def _():
-            fwd.x_arrive(3)
-
-        @pl.when(u == 3)
-        def _():
-            fwd.x_arrive(2)
-
-        for when, done in ((4, 1), (6, 3), (7, 2)):
+            sg_ref[h, :, place] = score_grad
+            key_more = jnp.dot(score_grad, q, preferred_element_type=F32)
+            value_more = jnp.dot(probs.astype(BF16), do, preferred_element_type=F32)
+            key_part = key_more if j == 0 else key_part + key_more
+            value_part = value_more if j == 0 else value_part + value_more
+        key_part = key_part * SCALE
+
+        for when, done in ((3, 1), (5, 2), (7, 3)):
             @pl.when(u == when)
             def _():
                 bwd.x_step(lax.rem(x + done, NX))
-
-        place = pl.ds(pl.multiple_of(half * HALF * HD, HALF * HD), HALF * HD)
-        key_part = jnp.dot(
-            sg_ref[h, :, place], jnp.concatenate(q, axis=0), preferred_element_type=F32
-        ) * SCALE
-        value_part = jnp.dot(
-            p_ref[...], jnp.concatenate(do, axis=0), preferred_element_type=F32
-        )
 
         @pl.when(half == 0)
         def _():
@@ -370,9 +378,10 @@
         kind = jnp.where(here, core, other)
         b = kind * KVH + lax.rem(x + i, NX)
 
-        @pl.when(here & (n > 0))
-        def _():
-            bwd.x_arrive(i)
+        for when, place in ((2, 1), (3, 3), (6, 2)):
+            @pl.when(n == when)
+            def _():
+                bwd.x_arrive(place)
 
         @pl.when(jnp.logical_not(here))
         def _():
@@ -397,12 +406,6 @@
 
     lax.fori_loop(0, 2 * KVH, y_loop, 0)
     vg_ref[0] = images[...].astype(BF16)
-
-    grad = yown[...]
-    for k in near_first(NY):
-        y_copy(k).wait_recv()
-        grad = grad + yrecv[k].astype(F32)
-    wg_ref[...] = grad
 
     for i in range(KVH):
         dq_copy(i).wait()
@@ -413,25 +416,18 @@
     for hop in (2, 6):
         w_third(hop).wait_send()
         w_fourth(hop).wait_send()
+
+    grad = yown[...]
+    for k in near_first(NY):
+        y_copy(k).wait_recv()
+        grad = grad + yrecv[k].astype(F32)
+    wg_ref[...] = grad
     for k in range(1, NY):
         y_copy(k).wait_send()
 
 
-def write(*refs):
-    sources, targets, sem = refs[:3], refs[3:6], refs[6]
-    copies = [
-        pltpu.make_async_copy(src, dst, sem.at[n])
-        for n, (src, dst) in enumerate(zip(sources, targets))
-    ]
-    for copy in copies:
-        copy.start()
-    for copy in copies:
-        copy.wait()
-
-
 def local(queries, out_grad, vision, w_kv, links, img_count):
     rows, width = queries.shape
-    anywhere = pl.BlockSpec(memory_space=pl.ANY)
     hbm = pl.BlockSpec(memory_space=pltpu.HBM)
     vmem = pl.BlockSpec(memory_space=pltpu.VMEM)
     sums = [
@@ -450,7 +446,7 @@
         jax.ShapeDtypeStruct(vision.shape, BF16),
         jax.ShapeDtypeStruct(w_kv.shape, F32),
     )
-    results = pl.pallas_call(
+    return pl.pallas_call(
         body,
         out_shape=out_shape,
         in_specs=[hbm] * 6,
@@ -461,11 +457,10 @@
             pltpu.VMEM((rows, width), BF16),
             pltpu.VMEM(vision.shape, BF16),
             pltpu.VMEM(link_slots.shape, jnp.int32),
-            pltpu.SMEM(img_count.shape, jnp.int32),
+            pltpu.VMEM((1, 1), jnp.int32),
             pltpu.VMEM((TOK, HD), F32),
             pltpu.VMEM((HD, TOK), BF16),
             pltpu.VMEM((NY, HD, HD), BF16),
-            pltpu.VMEM((TOK, GROUP // 2 * HD), BF16),
             pltpu.VMEM((KVH, TOK, GROUP * HD), BF16),
             pltpu.VMEM((KVH, 2, TOK, HD), F32),
             pltpu.VMEM((TOK, HD), F32),
@@ -482,15 +477,7 @@
         compiler_params=pltpu.CompilerParams(
             collective_id=0, has_side_effects=True, vmem_limit_bytes=60 * 1024 * 1024
         ),
-    )(queries, out_grad, vision, w_kv, link_slots, img_count)
-    return pl.pallas_call(
-        write,
-        out_shape=out_shape,
-        in_specs=[anywhere] * 3,
-        out_specs=(hbm,) * 3,
-        scratch_shapes=[pltpu.SemaphoreType.DMA((3,))],
-        compiler_params=pltpu.CompilerParams(vmem_limit_bytes=60 * 1024 * 1024),
-    )(*results)
+    )(queries, out_grad, vision, w_kv, link_slots, img_count.reshape(1, 1))
 
 
 def solution(mesh):

time: 121 us -> 86.9 us (0.72)
  the two profiles are of different devices: /device:TPU:17 before, /device:TPU:15 now
where the time goes in v3:
time: 86.9 us; the launch traced here: 86.7 us
  Pallas kernels  81.6 us (94%)
  local copies, waits for them, and re-layouts  3.82 us (4%)
  between operations  1.3 us (1%)
    pallas_call x1, Pallas kernels, local(): pl.pallas_call(body, out_shape=out_shape, in_specs=[hbm] * 6, out_specs=(...  81.6 us
    unnamed x7, local copies, waits for them, and re-layouts  3.82 us

profile of v3, /device:TPU:15, one launch (start us, length us, event | category | flops | bytes accessed | tf_op | source)
XLA Modules:
  0.0 86.7 jit_solution(1801036352281984719)
XLA Ops:
  1.3 81.6 %shard_map.85 = (bf16[128,4096]{1,0:T(8,128)(2,1)}, bf16[1,384,128]{2,1,0:T(8,128)(2,1)}, f32[128,128]{1,0:T(8,128)}) custom-call(bf16[128,4096]{1,0:T(8,128)(2,1)} %q_hbm.1, bf16[128,4096]{1,0:T(8,128)(2,1)} %do_hbm.1, bf16[1,384,128]{2,1,0:T(8,128)(2,1)} %vision_hbm.1, bf16[128,128]{1,0:T(8,128)(2,1)} %w_hbm.1, s32[1,16,64]{2,1,0:T(8,128)} %bitcast.3, ...), custom_call_target="tpu_custom_call" | custom-call | tf_op jit(solution)/shard_map/pallas_call | solution.py:449
  82.9 0.0 copy-start
  82.9 2.3 %copy.13 = bf16[128,4096]{1,0:T(8,128)(2,1)} copy(bf16[128,4096]{1,0:T(8,128)(2,1)} %get-tuple-element.6) | data formatting | bytes 2097152
  85.2 0.0 copy-done
  85.2 0.0 copy-start.1
  85.2 0.6 copy.14
  85.9 0.2 copy-done.1
  86.1 0.6 copy.15
Async XLA Ops:
  82.9 2.3 %copy-start = (bf16[1,384,128]{2,1,0:T(8,128)(2,1)S(1)}, bf16[1,384,128]{2,1,0:T(8,128)(2,1)}, u32[]{:S(2)}) copy-start(bf16[1,384,128]{2,1,0:T(8,128)(2,1)} %get-tuple-element.7) | copy-start | bytes 294916
  85.2 0.9 copy-start.1

commit v4 on v3

v4 whole, which is shorter than its diff:
```python
import jax
import jax.numpy as jnp
from jax import lax
from jax.experimental import pallas as pl
from jax.experimental.pallas import tpu as pltpu
from jax.sharding import PartitionSpec as P

HD = 128
QH = 32
KVH = 4
GROUP = QH // KVH
IMG_DOC = 16
IMG_LEN = 24
TOK = IMG_DOC * IMG_LEN
NZ, NX, NY = 8, 4, 8
PIECE = TOK // NZ
SCALE = HD ** (-0.5)
LOG2E = 1.4426950408889634
MESH = pl.DeviceIdType.MESH
F32, BF16 = jnp.float32, jnp.bfloat16

CORE, XS, ZS, AZ, AX, AC = 0, 4, 8, 16, 24, 29
FWD, BWD, WG, YS, VS, VG = 0, 33, 66, 84, 92, 93
SEMS = 94


def near_first(n):
    return sorted(range(1, n), key=lambda k: min(k, n - k))


def far_first(n):
    return near_first(n)[::-1]


def body(
    q_hbm, do_hbm, vision_hbm, w_hbm, links_hbm, count_hbm,
    dq_ref, vg_ref, wg_ref,
    q_ref, do_ref, vision_ref, links_ref, count_ref, bias_ref, vt_ref, w_all, vg_send, vg_recv,
    sg_ref, grads, images,
    xsend1, xrecv1, xown1, zsend1, zrecv1, kv1,
    csend, crecv, xsend2, xrecv2, xown2, zsend2, zrecv2, kv2,
    ysend, yrecv, yown,
    ssem, rsem, lsem,
):
    v = lax.axis_index("vis")
    t = lax.axis_index("txt")
    core = lax.rem(v, 2)
    x = lax.rem(lax.div(v, 2), NX)
    z = lax.div(v, 2 * NX)
    other = 1 - core
    mine = core * KVH + x

    def vis_at(zz, xx, cc):
        return (zz * NX + xx) * 2 + cc

    partner = (vis_at(z, x, other), t)

    def x_dev(k):
        return (vis_at(z, lax.rem(x + k, NX), core), t)

    def z_dev(k):
        return (vis_at(lax.rem(z + k, NZ), x, core), t)

    def y_dev(k, cc=core):
        return (vis_at(z, x, cc), lax.rem(t + k, NY))

    def piece(zz):
        return pl.ds(pl.multiple_of(zz * PIECE, PIECE), PIECE)

    def link(src, dst, sem, dev, arrival=None):
        return pltpu.make_async_remote_copy(
            src_ref=src, dst_ref=dst, send_sem=ssem.at[sem],
            recv_sem=rsem.at[sem if arrival is None else arrival],
            device_id=dev, device_id_type=MESH,
        )

    fetches = [
        pltpu.make_async_copy(src, dst, lsem.at[n])
        for n, (src, dst) in enumerate([
            (vision_hbm.at[0], vision_ref.at[core]), (links_hbm, links_ref),
            (count_hbm, count_ref), (q_hbm, q_ref), (do_hbm, do_ref),
        ])
    ]
    for fetch in fetches:
        fetch.start()

    barrier = pltpu.get_barrier_semaphore()
    partners = (
        [partner]
        + [x_dev(k) for k in range(1, NX)]
        + [z_dev(k) for k in range(1, NZ)]
        + [y_dev(k, cc) for k in range(1, NY) for cc in (core, other)]
    )
    for dev in partners:
        pl.semaphore_signal(barrier, inc=1, device_id=dev, device_id_type=MESH)
    pl.semaphore_wait(barrier, len(partners))

    kind_here = lax.div(t, KVH)

    def w_slot(b, cc, low=0, size=HD):
        rows = pl.ds(pl.multiple_of(cc * HD + low, HD // 2), size)
        return w_all.at[lax.rem(b, KVH), rows, :]

    def w_copy(k):
        place = WG + (NY - k if k else 0) * 2
        return link(w_hbm, w_slot(t, core), place + core, y_dev(k, kind_here), place + core)

    def w_third(j, cc):
        slot = w_slot(lax.rem(t + j, NY), cc)
        up = j == 2
        return link(slot, slot, WG + (3 if up else 5) * 2 + cc, y_dev(NY - 1 if up else 1))

    def w_fourth(j, cc):
        up = j == 2
        slot = w_slot(lax.rem(t + j, NY), cc, 0 if up else HD // 2, HD // 2)
        return link(slot, slot, WG + (4 if up else 8) * 2 + cc, y_dev(NY - 2 if up else 2))

    vision_copy = link(vision_hbm.at[0], vision_ref.at[core], VS, partner)
    w_here = pltpu.make_async_copy(w_hbm, w_slot(t, core), lsem.at[5])
    near_w = (1, NY - 1, 2, NY - 2)

    for k in near_w:
        w_copy(k).start()

    @pl.when(kind_here == core)
    def _():
        w_here.start()

    @pl.when(kind_here != core)
    def _():
        w_copy(0).start()

    vision_copy.start()
    for fetch in fetches[:3]:
        fetch.wait()

    block = lax.broadcasted_iota(jnp.int32, links_ref.shape[1:], 1)
    slot = lax.broadcasted_iota(jnp.int32, (IMG_DOC, 1), 0)
    linked = jnp.sum(jnp.where(block == v, links_ref[0], 0), axis=1, keepdims=True)
    bias = jnp.where((linked == 1) & (slot < count_ref[...]), 0.0, -1e30)
    for s in range(IMG_DOC):
        bias_ref[s * IMG_LEN : (s + 1) * IMG_LEN, :] = jnp.broadcast_to(
            bias[s : s + 1, :], (IMG_LEN, HD)
        )

    class Sums:
        def __init__(self, base, xsend, xrecv, xown, zsend, zrecv, kv):
            self.base = base
            self.xsend, self.xrecv, self.xown = xsend, xrecv, xown
            self.zsend, self.zrecv, self.kv = zsend, zrecv, kv

        def x_copy(self, k):
            return link(self.xsend.at[k], self.xrecv.at[k], self.base + XS + k, x_dev(k))

        def z_copy(self, k):
            rows = piece(lax.rem(z + k, NZ))
            return link(self.zsend.at[rows, :], self.zrecv.at[k], self.base + ZS + k, z_dev(k))

        def az_copy(self, k, zz):
            ref = self.kv.at[mine, piece(zz), :]
            return link(ref, ref, self.base + AZ + k, z_dev(k))

        def ax_copy(self, k, h):
            ref = self.kv.at[core * KVH + h]
            return link(ref, ref, self.base + AX + k, x_dev(k))

        def across(self, i):
            h = lax.rem(x + i, NX)
            up = i == 1
            half = self.kv.at[core * KVH + h, pl.ds(0 if up else TOK // 2, TOK // 2), :]
            return link(half, half, self.base + AX + (2 if up else 4), x_dev(3 if up else 1))

        def ac_copy(self, kind, h):
            ref = self.kv.at[kind * KVH + h]
            return link(ref, ref, self.base + AC + h, partner)

        def x_step(self, h, total):
            k = lax.rem(h - x + NX, NX)

            @pl.when(k == 0)
            def _():
                self.xown[...] = total

            @pl.when(k != 0)
            def _():
                self.xsend[k] = total.astype(BF16)
                self.x_copy(k).start()

        def z_stage(self, first=lambda: None, second=lambda: None, share=False):
            total = self.xown[...]
            for k in near_first(NX):
                self.x_copy(k).wait_recv()
                total = total + self.xrecv[k].astype(F32)
            self.xown[...] = total
            self.zsend[...] = total.astype(BF16)
            for k in far_first(NZ):
                self.z_copy(k).start()
            first()
            part = self.xown[piece(z), :]
            for k in near_first(NZ):
                self.z_copy(k).wait_recv()
                part = part + self.zrecv[k].astype(F32)
            self.kv[mine, piece(z), :] = part.astype(BF16)
            for k in far_first(NZ):
                self.az_copy(k, z).start()
            second()
            for k in near_first(NZ):
                self.az_copy(k, lax.rem(z - k + NZ, NZ)).wait_recv()
            if share:
                self.ac_copy(core, x).start()
            for k in (1, 3):
                self.ax_copy(k, x).start()

        def x_arrive(self, i, share=False):
            h = lax.rem(x + i, NX)
            if i == 2:
                for place, low in ((2, 0), (4, TOK // 2)):
                    half = self.kv.at[core * KVH + h, pl.ds(low, TOK // 2), :]
                    link(half, half, self.base + AX + place, x_dev(1)).wait_recv()
            else:
                self.ax_copy(NX - i, h).wait_recv()
                self.across(i).start()
            if share:
                self.ac_copy(core, h).start()

        def partner_arrive(self, i):
            self.ac_copy(other, lax.rem(x + i, NX)).wait_recv()

        def sent(self):
            for k in range(1, NX):
                self.x_copy(k).wait_send()
            for k in (1, 3):
                self.ax_copy(k, x).wait_send()
                self.across(k).wait_send()
            for k in range(1, NZ):
                self.z_copy(k).wait_send()
                self.az_copy(k, z).wait_send()

    fwd = Sums(FWD, xsend1, xrecv1, xown1, zsend1, zrecv1, kv1)
    bwd = Sums(BWD, xsend2, xrecv2, xown2, zsend2, zrecv2, kv2)

    def near(n):
        far = lax.div(n + 1, 2)
        return jnp.where(lax.rem(n, 2) == 1, far, lax.rem(NY - far, NY))

    vision_copy.wait_recv()
    vt_ref[:HD, :] = vision_ref[0].T
    vt_ref[HD:, :] = vision_ref[1].T

    def w_loop(n, carry):
        j = near(n)
        b = lax.rem(t + j, NY)
        h = lax.rem(b, KVH)

        @pl.when(lax.div(b, KVH) == core)
        def _():
            @pl.when(j == 0)
            def _():
                w_here.wait()
                link(w_hbm, w_slot(b, other), WG + other, partner).wait_recv()

            for cc in range(2):
                @pl.when((j != 0) & (j != 4))
                def _():
                    link(w_hbm, w_slot(b, cc), WG + j * 2 + cc, partner).wait_recv()

                for hop in (2, 6):
                    @pl.when(j == hop)
                    def _():
                        w_third(hop, cc).start()
                        w_fourth(hop, cc).start()

                @pl.when(j == 4)
                def _():
                    for place, low in ((4, 0), (8, HD // 2)):
                        half = w_slot(b, cc, low, HD // 2)
                        link(half, half, WG + place * 2 + cc, partner).wait_recv()

            images = jnp.concatenate([vision_ref[0], vision_ref[1]], axis=1)
            part = jnp.dot(images, w_all[h], preferred_element_type=F32)
            fwd.x_step(h, part)

        return carry

    lax.fori_loop(0, NY, w_loop, 0)
    fwd.z_stage(share=True)

    for fetch in fetches[3:]:
        fetch.wait()

    def core_copy(h):
        return link(csend.at[h], crecv.at[h], BWD + CORE + h, partner)

    def head_step(h):
        core_copy(h).wait_recv()
        bwd.x_step(h, grads[h, core] + crecv[h].astype(F32))

    HALF = GROUP // 2

    def attend(u, carry):
        mine_now = (u == 0) | (u == 2 * KVH - 1)
        i = jnp.where(mine_now, 0, lax.div(u + 1, 2))
        half = jnp.where(mine_now, lax.div(u, 2 * KVH - 1), lax.rem(u + 1, 2))
        h = lax.rem(x + i, NX)
        base = h * GROUP * HD + half * HALF * HD

        def columns(j):
            return pl.ds(pl.multiple_of(base + j * HD, HD), HD)

        @pl.when(u == 1)
        def _():
            fwd.x_arrive(1, share=True)
            fwd.x_arrive(3, share=True)

        @pl.when(u == 2)
        def _():
            fwd.x_arrive(2, share=True)

        @pl.when(half == 0)
        def _():
            fwd.partner_arrive(i)

        dims = (((1,), (1,)), ((), ()))
        bias = jnp.concatenate([bias_ref[...]] * 2, axis=1)
        key_part = value_part = None
        for j in range(0, HALF, 2):
            q = jnp.concatenate([q_ref[:, columns(j)], q_ref[:, columns(j + 1)]], axis=0)
            do = jnp.concatenate([do_ref[:, columns(j)], do_ref[:, columns(j + 1)]], axis=0)
            s = lax.dot_general(kv1[h], q, dims, preferred_element_type=F32)
            g = lax.dot_general(kv1[KVH + h], do, dims, preferred_element_type=F32)
            s = s * (SCALE * LOG2E) + bias
            e = jnp.exp2(s - jnp.max(s, axis=0, keepdims=True))
            norm = 1.0 / jnp.sum(e, axis=0, keepdims=True)
            delta = jnp.sum(e * g, axis=0, keepdims=True) * norm
            probs = e * norm
            score_grad = (probs * (g - delta)).astype(BF16)
            place = pl.ds(pl.multiple_of((half * HALF + j) * HD, HD), 2 * HD)
            sg_ref[h, :, place] = score_grad
            key_more = jnp.dot(score_grad, q, preferred_element_type=F32)
            value_more = jnp.dot(probs.astype(BF16), do, preferred_element_type=F32)
            key_part = key_more if j == 0 else key_part + key_more
            value_part = value_more if j == 0 else value_part + value_more
        key_part = key_part * SCALE

        for when, done in ((3, 1), (5, 2), (7, 3)):
            @pl.when(u == when)
            def _():
                head_step(lax.rem(x + done, NX))

        @pl.when(half == 0)
        def _():
            grads[h, 0] = key_part
            grads[h, 1] = value_part

        @pl.when(half == 1)
        def _():
            grads[h, 0] += key_part
            grads[h, 1] += value_part
            csend[h] = grads[h, other].astype(BF16)
            core_copy(h).start()

        return carry

    lax.fori_loop(0, 2 * KVH, attend, 0)

    def query_grads(low, high):
        def one(i, carry):
            h = lax.rem(x + i, NX)
            dq = jnp.dot(kv1[h].T, sg_ref[h], preferred_element_type=F32) * SCALE
            for j in range(GROUP):
                place = pl.ds(pl.multiple_of((h * GROUP + j) * HD, HD), HD)
                dq_ref[:, place] = dq[:, j * HD : (j + 1) * HD].T.astype(BF16)
            return carry

        lax.fori_loop(low, high, one, 0)

    query_grads(0, 1)
    head_step(x)
    bwd.z_stage(lambda: query_grads(1, KVH))

    def y_copy(h, cc):
        k = lax.rem(core * KVH + h - t + NY, NY)
        return link(ysend.at[h, cc], yrecv.at[k], YS + h * 2 + cc, y_dev(k, cc), YS + k)

    images[...] = jnp.zeros((TOK, 2 * HD), F32)

    def y_loop(n, carry):
        i = jnp.where(n < 2, n, 5 - n)
        h = lax.rem(x + i, NX)
        b = core * KVH + h

        for when, place in ((1, 1), (2, 3), (3, 2)):
            @pl.when(n == when)
            def _():
                bwd.x_arrive(place)

        part = jnp.dot(vt_ref[...], kv2[b], preferred_element_type=F32)
        for cc in range(2):
            share = part[cc * HD : (cc + 1) * HD, :]

            @pl.when((b == t) & (core == cc))
            def _():
                yown[...] = share

            @pl.when((b != t) | (core != cc))
            def _():
                ysend[h, cc] = share.astype(BF16)
                y_copy(h, cc).start()

        images[...] += lax.dot_general(
            kv2[b], w_all[h], (((1,), (1,)), ((), ())), preferred_element_type=F32
        )
        return carry

    lax.fori_loop(0, KVH, y_loop, 0)

    vg_copy = link(vg_send, vg_recv, VG, partner)

    def half_of_images(first):
        low, high = images[:, :HD], images[:, HD:]
        return jnp.where(first == 0, low, high)

    vg_send[...] = half_of_images(other).astype(BF16)
    vg_copy.start()

    fwd.sent()
    bwd.sent()
    for h in range(KVH):
        fwd.ac_copy(core, h).wait_send()
        core_copy(h).wait_send()
    vision_copy.wait_send()
    for k in near_w:
        w_copy(k).wait_send()

    @pl.when(kind_here != core)
    def _():
        w_copy(0).wait_send()

    for hop in (2, 6):
        @pl.when(lax.div(lax.rem(t + hop, NY), KVH) == core)
        def _():
            for cc in range(2):
                w_third(hop, cc).wait_send()
                w_fourth(hop, cc).wait_send()

    vg_copy.wait_recv()
    vg_ref[0] = (half_of_images(core) + vg_recv[...].astype(F32)).astype(BF16)

    @pl.when(kind_here != core)
    def _():
        link(ysend.at[0, 0], yrecv.at[0], YS, partner).wait_recv()
        yown[...] = yrecv[0].astype(F32)

    grad = yown[...]
    for k in near_first(NY):
        link(ysend.at[0, 0], yrecv.at[k], YS + k, partner).wait_recv()
        grad = grad + yrecv[k].astype(F32)
    wg_ref[...] = grad
    vg_copy.wait_send()
    for h in range(KVH):
        for cc in range(2):
            @pl.when((core * KVH + h != t) | (core != cc))
            def _():
                y_copy(h, cc).wait_send()


def write(*refs):
    sources, targets, sem = refs[:3], refs[3:6], refs[6]
    copies = [
        pltpu.make_async_copy(src, dst, sem.at[n])
        for n, (src, dst) in enumerate(zip(sources, targets))
    ]
    for copy in copies:
        copy.start()
    for copy in copies:
        copy.wait()


def local(queries, out_grad, vision, w_kv, links, img_count):
    rows, width = queries.shape
    hbm = pl.BlockSpec(memory_space=pltpu.HBM)
    vmem = pl.BlockSpec(memory_space=pltpu.VMEM)
    sums = [
        pltpu.VMEM((NX, TOK, HD), BF16),
        pltpu.VMEM((NX, TOK, HD), BF16),
        pltpu.VMEM((TOK, HD), F32),
        pltpu.VMEM((TOK, HD), BF16),
        pltpu.VMEM((NZ, PIECE, HD), BF16),
        pltpu.VMEM((2 * KVH, TOK, HD), BF16),
    ]
    link_slots = jnp.swapaxes(links, 1, 2)
    out_shape = (
        pltpu.VMEM(queries.shape, BF16),
        pltpu.VMEM(vision.shape, BF16),
        pltpu.VMEM(w_kv.shape, F32),
    )
    results = pl.pallas_call(
        body,
        out_shape=out_shape,
        in_specs=[hbm] * 6,
        out_specs=(vmem, vmem, vmem),
        scratch_shapes=[
            pltpu.VMEM((rows, width), BF16),
            pltpu.VMEM((rows, width), BF16),
            pltpu.VMEM((2, TOK, HD), BF16),
            pltpu.VMEM(link_slots.shape, jnp.int32),
            pltpu.VMEM((1, 1), jnp.int32),
            pltpu.VMEM((TOK, HD), F32),
            pltpu.VMEM((2 * HD, TOK), BF16),
            pltpu.VMEM((KVH, 2 * HD, HD), BF16),
            pltpu.VMEM((TOK, HD), BF16),
            pltpu.VMEM((TOK, HD), BF16),
            pltpu.VMEM((KVH, TOK, GROUP * HD), BF16),
            pltpu.VMEM((KVH, 2, TOK, HD), F32),
            pltpu.VMEM((TOK, 2 * HD), F32),
            *sums,
            pltpu.VMEM((KVH, TOK, HD), BF16),
            pltpu.VMEM((KVH, TOK, HD), BF16),
            *sums,
            pltpu.VMEM((KVH, 2, HD, HD), BF16),
            pltpu.VMEM((NY, HD, HD), BF16),
            pltpu.VMEM((HD, HD), F32),
            pltpu.SemaphoreType.DMA((SEMS,)),
            pltpu.SemaphoreType.DMA((SEMS,)),
            pltpu.SemaphoreType.DMA((6,)),
        ],
        compiler_params=pltpu.CompilerParams(
            collective_id=0, has_side_effects=True, vmem_limit_bytes=40 * 1024 * 1024
        ),
    )(*[
        pltpu.with_memory_space_constraint(a, pltpu.HBM)
        for a in (queries, out_grad, vision, w_kv, link_slots)
    ], img_count.reshape(1, 1))
    return pl.pallas_call(
        write,
        out_shape=tuple(jax.ShapeDtypeStruct(r.shape, r.dtype) for r in results),
        in_specs=[vmem] * 3,
        out_specs=(hbm,) * 3,
        scratch_shapes=[pltpu.SemaphoreType.DMA((3,))],
    )(*results)


def solution(mesh):
    in_specs = (
        P(("txt", "vis"), None),
        P(("txt", "vis"), None),
        P("txt", None, "vis"),
        P("vis", "txt"),
        P("txt", None, None),
        P("txt"),
    )
    out_specs = (P(("txt", "vis"), None), P("txt", None, "vis"), P("vis", "txt"))
    return jax.shard_map(local, mesh=mesh, in_specs=in_specs, out_specs=out_specs, check_vma=False)
```

time: 86.9 us -> 87.1 us (level)
  Pallas kernels: 81.6 us -> 83.4 us
  local copies, waits for them, and re-layouts: 3.82 us -> 2.21 us
    pallas_call x0 -> x1, Pallas kernels: none -> 2.32 us  [local(): pl.pallas_call(write, out_shape=tuple((jax.ShapeDtypeStruct(r.shape, r.dt...]
    unnamed x7 -> x6, local copies, waits for them, and re-layouts: 3.82 us -> 2.21 us
where the time goes in v4:
time: 87.1 us; the launch traced here: 86.9 us
  Pallas kernels  83.4 us (96%)
  local copies, waits for them, and re-layouts  2.21 us (3%)
  between operations  1.3 us (1%)
    pallas_call x1, Pallas kernels, local(): pl.pallas_call(body, out_shape=out_shape, in_specs=[hbm] * 6, out_specs=(...  81 us
    pallas_call x1, Pallas kernels, local(): pl.pallas_call(write, out_shape=tuple((jax.ShapeDtypeStruct(r.shape, r.dt...  2.32 us
    unnamed x6, local copies, waits for them, and re-layouts  2.21 us

profile of v4, /device:TPU:15, one launch (start us, length us, event | category | flops | bytes accessed | tf_op | source)
XLA Modules:
  0.0 86.9 jit_solution(2156189747309935366)
XLA Ops:
  1.3 81.0 %shard_map.85 = (bf16[128,4096]{1,0:T(8,128)(2,1)S(1)}, bf16[1,384,128]{2,1,0:T(8,128)(2,1)S(1)}, f32[128,128]{1,0:T(8,128)S(1)}) custom-call(bf16[128,4096]{1,0:T(8,128)(2,1)} %q_hbm.1, bf16[128,4096]{1,0:T(8,128)(2,1)} %do_hbm.1, bf16[1,384,128]{2,1,0:T(8,128)(2,1)} %vision_hbm.1, bf16[128,128]{1,0:T(8,128)(2,1)} %w_hbm.1, s32[1,16,64]{2,1,0:T(8,128)} %bitcast.3, ...), custom_call_target="tpu_custom_call" | custom-call | tf_op jit(solution)/shard_map/pallas_call | solution.py:497
  82.3 0.0 copy-start
  82.3 1.0 %copy-done = bf16[128,4096]{1,0:T(8,128)(2,1)} copy-done((bf16[128,4096]{1,0:T(8,128)(2,1)}, bf16[128,4096]{1,0:T(8,128)(2,1)S(1)}, u32[]{:S(2)}) %copy-start) | copy-done | bytes 1048600
  83.3 0.0 copy-start.1
  83.3 0.6 copy-done.1
  83.9 0.0 copy-start.2
  83.9 0.6 copy-done.2
  84.5 2.3 %shard_map.86 = (bf16[128,4096]{1,0:T(8,128)(2,1)}, bf16[1,384,128]{2,1,0:T(8,128)(2,1)}, f32[128,128]{1,0:T(8,128)}) custom-call(bf16[128,4096]{1,0:T(8,128)(2,1)} %copy-done, bf16[1,384,128]{2,1,0:T(8,128)(2,1)} %copy-done.1, f32[128,128]{1,0:T(8,128)} %copy-done.2), custom_call_target="tpu_custom_call" | custom-call | tf_op jit(solution)/shard_map/pallas_call | solution.py:534
Async XLA Ops:
  82.3 1.0 %copy-start = (bf16[128,4096]{1,0:T(8,128)(2,1)}, bf16[128,4096]{1,0:T(8,128)(2,1)S(1)}, u32[]{:S(2)}) copy-start(bf16[128,4096]{1,0:T(8,128)(2,1)S(1)} %get-tuple-element.6.refs_0_) | copy-start | bytes 3145732
  83.3 0.6 copy-start.1
  83.9 0.6 copy-start.2

commit v5 on v4

--- a/solution.py
+++ b/solution.py
@@ -86,10 +86,10 @@
 
     barrier = pltpu.get_barrier_semaphore()
     partners = (
-        [partner]
-        + [x_dev(k) for k in range(1, NX)]
-        + [z_dev(k) for k in range(1, NZ)]
-        + [y_dev(k, cc) for k in range(1, NY) for cc in (core, other)]
+        [y_dev(k, cc) for k in far_first(NY) for cc in (core, other)]
+        + [z_dev(k) for k in far_first(NZ)]
+        + [x_dev(k) for k in far_first(NX)]
+        + [partner]
     )
     for dev in partners:
         pl.semaphore_signal(barrier, inc=1, device_id=dev, device_id_type=MESH)
@@ -374,9 +374,10 @@
 
         lax.fori_loop(low, high, one, 0)
 
-    query_grads(0, 1)
+    ahead = 2 * core
+    query_grads(0, ahead)
     head_step(x)
-    bwd.z_stage(lambda: query_grads(1, KVH))
+    bwd.z_stage(lambda: query_grads(ahead, KVH))
 
     def y_copy(h, cc):
         k = lax.rem(core * KVH + h - t + NY, NY)
@@ -537,7 +538,8 @@
         in_specs=[vmem] * 3,
         out_specs=(hbm,) * 3,
         scratch_shapes=[pltpu.SemaphoreType.DMA((3,))],
-    )(*results)
+        compiler_params=pltpu.CompilerParams(vmem_limit_bytes=4 * 1024 * 1024),
+    )(*[pltpu.with_memory_space_constraint(a, pltpu.VMEM) for a in results])
 
 
 def solution(mesh):

time: 87.1 us -> 83.5 us (0.959)
  local copies, waits for them, and re-layouts: 2.21 us -> 0 us
  Pallas kernels: 83.4 us -> 82 us
    unnamed x6 -> x0, local copies, waits for them, and re-layouts: 2.21 us -> none
    pallas_call x1, Pallas kernels: 2.32 us -> 1.04 us  [local(): pl.pallas_call(write, out_shape=tuple((jax.ShapeDtypeStruct(r.shape, r.dt...]
where the time goes in v5:
time: 83.5 us; the launch traced here: 83.3 us
  Pallas kernels  82 us (98%)
  between operations  1.29 us (2%)
    pallas_call x1, Pallas kernels, local(): pl.pallas_call(body, out_shape=out_shape, in_specs=[hbm] * 6, out_specs=(...  81 us

profile of v5, /device:TPU:15, one launch (start us, length us, event | category | flops | bytes accessed | tf_op | source)
XLA Modules:
  0.0 83.3 jit_solution(16702465374729106313)
XLA Ops:
  1.3 81.0 %shard_map.85 = (bf16[128,4096]{1,0:T(8,128)(2,1)S(1)}, bf16[1,384,128]{2,1,0:T(8,128)(2,1)S(1)}, f32[128,128]{1,0:T(8,128)S(1)}) custom-call(bf16[128,4096]{1,0:T(8,128)(2,1)} %q_hbm.1, bf16[128,4096]{1,0:T(8,128)(2,1)} %do_hbm.1, bf16[1,384,128]{2,1,0:T(8,128)(2,1)} %vision_hbm.1, bf16[128,128]{1,0:T(8,128)(2,1)} %w_hbm.1, s32[1,16,64]{2,1,0:T(8,128)} %bitcast.3, ...), custom_call_target="tpu_custom_call" | custom-call | tf_op jit(solution)/shard_map/pallas_call | solution.py:498
  82.3 1.0 %shard_map.86 = (bf16[128,4096]{1,0:T(8,128)(2,1)}, bf16[1,384,128]{2,1,0:T(8,128)(2,1)}, f32[128,128]{1,0:T(8,128)}) custom-call(bf16[128,4096]{1,0:T(8,128)(2,1)S(1)} %get-tuple-element.6.refs_0_, bf16[1,384,128]{2,1,0:T(8,128)(2,1)S(1)} %get-tuple-element.7.refs_1_, f32[128,128]{1,0:T(8,128)S(1)} %get-tuple-element.8.refs_2_), custom_call_target="tpu_custom_call" | custom-call | tf_op jit(solution)/shard_map/pallas_call | solution.py:535

commit v6 on v5

--- a/solution.py
+++ b/solution.py
@@ -19,9 +19,9 @@
 MESH = pl.DeviceIdType.MESH
 F32, BF16 = jnp.float32, jnp.bfloat16
 
-CORE, XS, ZS, AZ, AX, AC = 0, 4, 8, 16, 24, 29
-FWD, BWD, WG, YS, VS, VG = 0, 33, 66, 84, 92, 93
-SEMS = 94
+CORE, XS, ZS, AZ, AX, AC, XZ = 0, 4, 8, 16, 24, 30, 34
+FWD, BWD, WG, YS, VS, VG = 0, 42, 84, 102, 110, 111
+SEMS = 112
 
 
 def near_first(n):
@@ -39,7 +39,7 @@
     sg_ref, grads, images,
     xsend1, xrecv1, xown1, zsend1, zrecv1, kv1,
     csend, crecv, xsend2, xrecv2, xown2, zsend2, zrecv2, kv2,
-    ysend, yrecv, yown,
+    xz_recv, ysend, yrecv, yown,
     ssem, rsem, lsem,
 ):
     v = lax.axis_index("vis")
@@ -61,6 +61,9 @@
     def z_dev(k):
         return (vis_at(lax.rem(z + k, NZ), x, core), t)
 
+    def xz_dev(i, k):
+        return (vis_at(lax.rem(z + k, NZ), lax.rem(x + i, NX), core), t)
+
     def y_dev(k, cc=core):
         return (vis_at(z, x, cc), lax.rem(t + k, NY))
 
@@ -90,6 +93,7 @@
         + [z_dev(k) for k in far_first(NZ)]
         + [x_dev(k) for k in far_first(NX)]
         + [partner]
+        + [xz_dev(1, k) for k in range(1, NZ)]
     )
     for dev in partners:
         pl.semaphore_signal(barrier, inc=1, device_id=dev, device_id_type=MESH)
@@ -160,15 +164,17 @@
             ref = self.kv.at[mine, piece(zz), :]
             return link(ref, ref, self.base + AZ + k, z_dev(k))
 
-        def ax_copy(self, k, h):
-            ref = self.kv.at[core * KVH + h]
-            return link(ref, ref, self.base + AX + k, x_dev(k))
+        def half_block(self, h, part):
+            return self.kv.at[core * KVH + h, pl.ds(part * (TOK // 2), TOK // 2), :]
+
+        def ax_copy(self, k, h, part):
+            half = self.half_block(h, part)
+            return link(half, half, self.base + AX + (k - 1) + part, x_dev(k))
 
         def across(self, i):
-            h = lax.rem(x + i, NX)
-            up = i == 1
-            half = self.kv.at[core * KVH + h, pl.ds(0 if up else TOK // 2, TOK // 2), :]
-            return link(half, half, self.base + AX + (2 if up else 4), x_dev(3 if up else 1))
+            part = 0 if i == 1 else 1
+            half = self.half_block(lax.rem(x + i, NX), part)
+            return link(half, half, self.base + AX + 4 + part, x_dev(NX - i))
 
         def ac_copy(self, kind, h):
             ref = self.kv.at[kind * KVH + h]
@@ -186,9 +192,9 @@
                 self.xsend[k] = total.astype(BF16)
                 self.x_copy(k).start()
 
-        def z_stage(self, first=lambda: None, second=lambda: None, share=False):
+        def z_stage(self, first=lambda: None, share=False, from_x=(1, 3, 2), more=lambda part: part):
             total = self.xown[...]
-            for k in near_first(NX):
+            for k in from_x:
                 self.x_copy(k).wait_recv()
                 total = total + self.xrecv[k].astype(F32)
             self.xown[...] = total
@@ -200,37 +206,41 @@
             for k in near_first(NZ):
                 self.z_copy(k).wait_recv()
                 part = part + self.zrecv[k].astype(F32)
-            self.kv[mine, piece(z), :] = part.astype(BF16)
+            self.kv[mine, piece(z), :] = more(part).astype(BF16)
             for k in far_first(NZ):
                 self.az_copy(k, z).start()
-            second()
             for k in near_first(NZ):
                 self.az_copy(k, lax.rem(z - k + NZ, NZ)).wait_recv()
             if share:
                 self.ac_copy(core, x).start()
-            for k in (1, 3):
-                self.ax_copy(k, x).start()
+            for k, half in ((3, 0), (1, 1), (3, 1), (1, 0)):
+                self.ax_copy(k, x, half).start()
+
+        def pass_on(self, i):
+            h = lax.rem(x + i, NX)
+            self.ax_copy(NX - i, h, 0 if i == 1 else 1).wait_recv()
+            self.across(i).start()
 
         def x_arrive(self, i, share=False):
             h = lax.rem(x + i, NX)
             if i == 2:
-                for place, low in ((2, 0), (4, TOK // 2)):
-                    half = self.kv.at[core * KVH + h, pl.ds(low, TOK // 2), :]
-                    link(half, half, self.base + AX + place, x_dev(1)).wait_recv()
+                for part in range(2):
+                    half = self.half_block(h, part)
+                    link(half, half, self.base + AX + 4 + part, x_dev(1)).wait_recv()
             else:
-                self.ax_copy(NX - i, h).wait_recv()
-                self.across(i).start()
+                self.ax_copy(NX - i, h, 1 if i == 1 else 0).wait_recv()
             if share:
                 self.ac_copy(core, h).start()
 
         def partner_arrive(self, i):
             self.ac_copy(other, lax.rem(x + i, NX)).wait_recv()
 
-        def sent(self):
-            for k in range(1, NX):
+        def sent(self, to_x=(1, 2, 3)):
+            for k in to_x:
                 self.x_copy(k).wait_send()
             for k in (1, 3):
-                self.ax_copy(k, x).wait_send()
+                for part in range(2):
+                    self.ax_copy(k, x, part).wait_send()
                 self.across(k).wait_send()
             for k in range(1, NZ):
                 self.z_copy(k).wait_send()
@@ -290,6 +300,23 @@
 
     def core_copy(h):
         return link(csend.at[h], crecv.at[h], BWD + CORE + h, partner)
+
+    def xz_copy(k):
+        rows = piece(lax.rem(z + k, NZ))
+        return link(xsend2.at[3, rows, :], xz_recv.at[k], BWD + XZ + k, xz_dev(3, k))
+
+    def last_step():
+        h = lax.rem(x + 3, NX)
+        core_copy(h).wait_recv()
+        xsend2[3] = (grads[h, core] + crecv[h].astype(F32)).astype(BF16)
+        for k in [*far_first(NZ), 0]:
+            xz_copy(k).start()
+
+    def last_arrive(part):
+        for k in [0, *near_first(NZ)]:
+            xz_copy(k).wait_recv()
+            part = part + xz_recv[k].astype(F32)
+        return part
 
     def head_step(h):
         core_copy(h).wait_recv()
@@ -309,6 +336,8 @@
 
         @pl.when(u == 1)
         def _():
+            fwd.pass_on(1)
+            fwd.pass_on(3)
             fwd.x_arrive(1, share=True)
             fwd.x_arrive(3, share=True)
 
@@ -342,11 +371,6 @@
             value_part = value_more if j == 0 else value_part + value_more
         key_part = key_part * SCALE
 
-        for when, done in ((3, 1), (5, 2), (7, 3)):
-            @pl.when(u == when)
-            def _():
-                head_step(lax.rem(x + done, NX))
-
         @pl.when(half == 0)
         def _():
             grads[h, 0] = key_part
@@ -359,9 +383,15 @@
             csend[h] = grads[h, other].astype(BF16)
             core_copy(h).start()
 
+        for when, done in ((3, 1), (5, 2)):
+            @pl.when(u == when)
+            def _():
+                head_step(lax.rem(x + done, NX))
+
         return carry
 
     lax.fori_loop(0, 2 * KVH, attend, 0)
+    last_step()
 
     def query_grads(low, high):
         def one(i, carry):
@@ -374,10 +404,9 @@
 
         lax.fori_loop(low, high, one, 0)
 
-    ahead = 2 * core
-    query_grads(0, ahead)
+    query_grads(0, 1)
     head_step(x)
-    bwd.z_stage(lambda: query_grads(ahead, KVH))
+    bwd.z_stage(lambda: query_grads(1, KVH), from_x=(1, 2), more=last_arrive)
 
     def y_copy(h, cc):
         k = lax.rem(core * KVH + h - t + NY, NY)
@@ -390,6 +419,11 @@
         h = lax.rem(x + i, NX)
         b = core * KVH + h
 
+        @pl.when(n == 1)
+        def _():
+            bwd.pass_on(1)
+            bwd.pass_on(3)
+
         for when, place in ((1, 1), (2, 3), (3, 2)):
             @pl.when(n == when)
             def _():
@@ -425,7 +459,9 @@
     vg_copy.start()
 
     fwd.sent()
-    bwd.sent()
+    bwd.sent(to_x=(1, 2))
+    for k in range(NZ):
+        xz_copy(k).wait_send()
     for h in range(KVH):
         fwd.ac_copy(core, h).wait_send()
         core_copy(h).wait_send()
@@ -518,6 +554,7 @@
             pltpu.VMEM((KVH, TOK, HD), BF16),
             pltpu.VMEM((KVH, TOK, HD), BF16),
             *sums,
+            pltpu.VMEM((NZ, PIECE, HD), BF16),
             pltpu.VMEM((KVH, 2, HD, HD), BF16),
             pltpu.VMEM((NY, HD, HD), BF16),
             pltpu.VMEM((HD, HD), F32),

time: 83.5 us -> 81.5 us (0.976)
  the two profiles are of different devices: /device:TPU:15 before, /device:TPU:17 now
where the time goes in v6:
time: 81.5 us; the launch traced here: 81.3 us
  Pallas kernels  80 us (98%)
  between operations  1.29 us (2%)
    pallas_call x1, Pallas kernels, local(): pl.pallas_call(body, out_shape=out_shape, in_specs=[hbm] * 6, out_specs=(...  79 us

profile of v6, /device:TPU:17, one launch (start us, length us, event | category | flops | bytes accessed | tf_op | source)
XLA Modules:
  0.0 81.3 jit_solution(2959032528704511905)
XLA Ops:
  1.3 79.0 %shard_map.85 = (bf16[128,4096]{1,0:T(8,128)(2,1)S(1)}, bf16[1,384,128]{2,1,0:T(8,128)(2,1)S(1)}, f32[128,128]{1,0:T(8,128)S(1)}) custom-call(bf16[128,4096]{1,0:T(8,128)(2,1)} %q_hbm.1, bf16[128,4096]{1,0:T(8,128)(2,1)} %do_hbm.1, bf16[1,384,128]{2,1,0:T(8,128)(2,1)} %vision_hbm.1, bf16[128,128]{1,0:T(8,128)(2,1)} %w_hbm.1, s32[1,16,64]{2,1,0:T(8,128)} %bitcast.3, ...), custom_call_target="tpu_custom_call" | custom-call | tf_op jit(solution)/shard_map/pallas_call | solution.py:534
  80.2 1.0 %shard_map.86 = (bf16[128,4096]{1,0:T(8,128)(2,1)}, bf16[1,384,128]{2,1,0:T(8,128)(2,1)}, f32[128,128]{1,0:T(8,128)}) custom-call(bf16[128,4096]{1,0:T(8,128)(2,1)S(1)} %get-tuple-element.6.refs_0_, bf16[1,384,128]{2,1,0:T(8,128)(2,1)S(1)} %get-tuple-element.7.refs_1_, f32[128,128]{1,0:T(8,128)S(1)} %get-tuple-element.8.refs_2_), custom_call_target="tpu_custom_call" | custom-call | tf_op jit(solution)/shard_map/pallas_call | solution.py:572

commit v7 on v6

--- a/solution.py
+++ b/solution.py
@@ -19,9 +19,9 @@
 MESH = pl.DeviceIdType.MESH
 F32, BF16 = jnp.float32, jnp.bfloat16
 
-CORE, XS, ZS, AZ, AX, AC, XZ = 0, 4, 8, 16, 24, 30, 34
-FWD, BWD, WG, YS, VS, VG = 0, 42, 84, 102, 110, 111
-SEMS = 112
+CORE, XS, ZS, AZ, AX, AC, XZ, OZ = 0, 4, 8, 16, 24, 30, 34, 42
+FWD, BWD, WG, YS, VS, VG = 0, 50, 100, 118, 126, 127
+SEMS = 128
 
 
 def near_first(n):
@@ -39,7 +39,7 @@
     sg_ref, grads, images,
     xsend1, xrecv1, xown1, zsend1, zrecv1, kv1,
     csend, crecv, xsend2, xrecv2, xown2, zsend2, zrecv2, kv2,
-    xz_recv, ysend, yrecv, yown,
+    xz_recv, oz_recv, ysend, yrecv, yown,
     ssem, rsem, lsem,
 ):
     v = lax.axis_index("vis")
@@ -64,6 +64,9 @@
     def xz_dev(i, k):
         return (vis_at(lax.rem(z + k, NZ), lax.rem(x + i, NX), core), t)
 
+    def oz_dev(k):
+        return (vis_at(lax.rem(z + k, NZ), x, other), t)
+
     def y_dev(k, cc=core):
         return (vis_at(z, x, cc), lax.rem(t + k, NY))
 
@@ -94,6 +97,7 @@
         + [x_dev(k) for k in far_first(NX)]
         + [partner]
         + [xz_dev(1, k) for k in range(1, NZ)]
+        + [oz_dev(k) for k in range(1, NZ)]
     )
     for dev in partners:
         pl.semaphore_signal(barrier, inc=1, device_id=dev, device_id_type=MESH)
@@ -312,7 +316,14 @@
         for k in [*far_first(NZ), 0]:
             xz_copy(k).start()
 
+    def oz_copy(k):
+        rows = piece(lax.rem(z + k, NZ))
+        return link(csend.at[x, rows, :], oz_recv.at[k], BWD + OZ + k, oz_dev(k))
+
     def last_arrive(part):
+        for k in [0, *near_first(NZ)]:
+            oz_copy(k).wait_recv()
+            part = part + oz_recv[k].astype(F32)
         for k in [0, *near_first(NZ)]:
             xz_copy(k).wait_recv()
             part = part + xz_recv[k].astype(F32)
@@ -381,7 +392,10 @@
             grads[h, 0] += key_part
             grads[h, 1] += value_part
             csend[h] = grads[h, other].astype(BF16)
-            core_copy(h).start()
+
+            @pl.when(u < 2 * KVH - 1)
+            def _():
+                core_copy(h).start()
 
         for when, done in ((3, 1), (5, 2)):
             @pl.when(u == when)
@@ -404,9 +418,10 @@
 
         lax.fori_loop(low, high, one, 0)
 
-    query_grads(0, 1)
-    head_step(x)
-    bwd.z_stage(lambda: query_grads(1, KVH), from_x=(1, 2), more=last_arrive)
+    for k in [*far_first(NZ), 0]:
+        oz_copy(k).start()
+    bwd.x_step(x, grads[x, core])
+    bwd.z_stage(lambda: query_grads(0, KVH), from_x=(1, 2), more=last_arrive)
 
     def y_copy(h, cc):
         k = lax.rem(core * KVH + h - t + NY, NY)
@@ -442,12 +457,17 @@
                 ysend[h, cc] = share.astype(BF16)
                 y_copy(h, cc).start()
 
+        return carry
+
+    lax.fori_loop(0, KVH, y_loop, 0)
+
+    def image_loop(h, carry):
         images[...] += lax.dot_general(
-            kv2[b], w_all[h], (((1,), (1,)), ((), ())), preferred_element_type=F32
+            kv2[core * KVH + h], w_all[h], (((1,), (1,)), ((), ())), preferred_element_type=F32
         )
         return carry
 
-    lax.fori_loop(0, KVH, y_loop, 0)
+    lax.fori_loop(0, KVH, image_loop, 0)
 
     vg_copy = link(vg_send, vg_recv, VG, partner)
 
@@ -462,9 +482,11 @@
     bwd.sent(to_x=(1, 2))
     for k in range(NZ):
         xz_copy(k).wait_send()
+        oz_copy(k).wait_send()
     for h in range(KVH):
         fwd.ac_copy(core, h).wait_send()
-        core_copy(h).wait_send()
+    for i in range(1, KVH):
+        core_copy(lax.rem(x + i, NX)).wait_send()
     vision_copy.wait_send()
     for k in near_w:
         w_copy(k).wait_send()
@@ -555,6 +577,7 @@
             pltpu.VMEM((KVH, TOK, HD), BF16),
             *sums,
             pltpu.VMEM((NZ, PIECE, HD), BF16),
+            pltpu.VMEM((NZ, PIECE, HD), BF16),
             pltpu.VMEM((KVH, 2, HD, HD), BF16),
             pltpu.VMEM((NY, HD, HD), BF16),
             pltpu.VMEM((HD, HD), F32),

time: 81.5 us -> 83.6 us (1.026)
  Pallas kernels: 80 us -> 82.2 us
    pallas_call x1, Pallas kernels: 79 us -> 81.1 us  [local(): pl.pallas_call(body, out_shape=out_shape, in_specs=[hbm] * 6, out_specs=(...]
where the time goes in v7:
time: 83.6 us; the launch traced here: 83.4 us
  Pallas kernels  82.2 us (98%)
  between operations  1.29 us (2%)
    pallas_call x1, Pallas kernels, local(): pl.pallas_call(body, out_shape=out_shape, in_specs=[hbm] * 6, out_specs=(...  81.1 us

profile of v7, /device:TPU:17, one launch (start us, length us, event | category | flops | bytes accessed | tf_op | source)
XLA Modules:
  0.0 83.4 jit_solution(18002513485372908598)
XLA Ops:
  1.3 81.1 %shard_map.85 = (bf16[128,4096]{1,0:T(8,128)(2,1)S(1)}, bf16[1,384,128]{2,1,0:T(8,128)(2,1)S(1)}, f32[128,128]{1,0:T(8,128)S(1)}) custom-call(bf16[128,4096]{1,0:T(8,128)(2,1)} %q_hbm.1, bf16[128,4096]{1,0:T(8,128)(2,1)} %do_hbm.1, bf16[1,384,128]{2,1,0:T(8,128)(2,1)} %vision_hbm.1, bf16[128,128]{1,0:T(8,128)(2,1)} %w_hbm.1, s32[1,16,64]{2,1,0:T(8,128)} %bitcast.3, ...), custom_call_target="tpu_custom_call" | custom-call | tf_op jit(solution)/shard_map/pallas_call | solution.py:556
  82.4 1.0 %shard_map.86 = (bf16[128,4096]{1,0:T(8,128)(2,1)}, bf16[1,384,128]{2,1,0:T(8,128)(2,1)}, f32[128,128]{1,0:T(8,128)}) custom-call(bf16[128,4096]{1,0:T(8,128)(2,1)S(1)} %get-tuple-element.6.refs_0_, bf16[1,384,128]{2,1,0:T(8,128)(2,1)S(1)} %get-tuple-element.7.refs_1_, f32[128,128]{1,0:T(8,128)S(1)} %get-tuple-element.8.refs_2_), custom_call_target="tpu_custom_call" | custom-call | tf_op jit(solution)/shard_map/pallas_call | solution.py:595

commit v8 on v6

--- a/solution.py
+++ b/solution.py
@@ -442,12 +442,17 @@
                 ysend[h, cc] = share.astype(BF16)
                 y_copy(h, cc).start()
 
+        return carry
+
+    lax.fori_loop(0, KVH, y_loop, 0)
+
+    def image_loop(h, carry):
         images[...] += lax.dot_general(
-            kv2[b], w_all[h], (((1,), (1,)), ((), ())), preferred_element_type=F32
+            kv2[core * KVH + h], w_all[h], (((1,), (1,)), ((), ())), preferred_element_type=F32
         )
         return carry
 
-    lax.fori_loop(0, KVH, y_loop, 0)
+    lax.fori_loop(0, KVH, image_loop, 0)
 
     vg_copy = link(vg_send, vg_recv, VG, partner)
 

time: 81.5 us -> 81.5 us (level)
  no operation moved by 1% of the time
where the time goes in v8:
time: 81.5 us; the launch traced here: 81.3 us
  Pallas kernels  80 us (98%)
  between operations  1.29 us (2%)
    pallas_call x1, Pallas kernels, local(): pl.pallas_call(body, out_shape=out_shape, in_specs=[hbm] * 6, out_specs=(...  78.9 us

profile of v8, /device:TPU:17, one launch (start us, length us, event | category | flops | bytes accessed | tf_op | source)
XLA Modules:
  0.0 81.3 jit_solution(2117481247699750790)
XLA Ops:
  1.3 78.9 %shard_map.85 = (bf16[128,4096]{1,0:T(8,128)(2,1)S(1)}, bf16[1,384,128]{2,1,0:T(8,128)(2,1)S(1)}, f32[128,128]{1,0:T(8,128)S(1)}) custom-call(bf16[128,4096]{1,0:T(8,128)(2,1)} %q_hbm.1, bf16[128,4096]{1,0:T(8,128)(2,1)} %do_hbm.1, bf16[1,384,128]{2,1,0:T(8,128)(2,1)} %vision_hbm.1, bf16[128,128]{1,0:T(8,128)(2,1)} %w_hbm.1, s32[1,16,64]{2,1,0:T(8,128)} %bitcast.3, ...), custom_call_target="tpu_custom_call" | custom-call | tf_op jit(solution)/shard_map/pallas_call | solution.py:539
  80.2 1.0 %shard_map.86 = (bf16[128,4096]{1,0:T(8,128)(2,1)}, bf16[1,384,128]{2,1,0:T(8,128)(2,1)}, f32[128,128]{1,0:T(8,128)}) custom-call(bf16[128,4096]{1,0:T(8,128)(2,1)S(1)} %get-tuple-element.6.refs_0_, bf16[1,384,128]{2,1,0:T(8,128)(2,1)S(1)} %get-tuple-element.7.refs_1_, f32[128,128]{1,0:T(8,128)S(1)} %get-tuple-element.8.refs_2_), custom_call_target="tpu_custom_call" | custom-call | tf_op jit(solution)/shard_map/pallas_call | solution.py:577
